TPU v7x, 256 devices: a whole 4x4x8 slice. The times are simulated.
256 devices in a mesh: row: 64 (over x, z, core), col: 4 (over y).
Axes of the slice: x: 4, y: 4, z: 8, core: 2. Of those that a mesh axis runs over, the one named last changes fastest.
Arguments:
- query_grads: bfloat16 [4, 8192, 28672], P(None, 'row', 'col'), may hold values from -0.00036621094 to 0.00036621094
- out_grads: bfloat16 [1024, 8192], P('col', 'row'), may hold values from -6 to 6
- activations: bfloat16 [1024, 28672], P('row', 'col'), may hold values from -6 to 6
- seq_ids: int32 [1024], P('row'), may hold values from 0 to 31, never falling along the last dimension, each value on 1 to 64 neighbouring positions
Outputs:
- scores: float32 [1024, 4], P('row')
- seq_scores: float32 [32, 4], replicated
Inputs may be any that keep to these rules, and one draw needn't show every extreme that they name: `seq_ids`: non-decreasing along the tokens; every sequence holds between 1 and 64 tokens.
All inputs are finite; a program needn't handle non-finite values.
Results may differ from a plain program's by a relative error of at most 0.0003.
Values may be sent and summed in bfloat16 or wider, within the bound.
No kernel may reach another device: no remote copies, remote signals or barrier semaphores. Data moves between devices by JAX's collectives and lax.ppermute only.
A program may use at most 64 MiB of HBM per device.

v0:
```python
import jax
import jax.numpy as jnp
from jax import lax
from jax.sharding import PartitionSpec as P


def block_scores(flat_grads, pieces, grad_slice, queries):
    inner = jnp.dot(flat_grads, pieces.T, preferred_element_type=jnp.float32)
    inner = inner.reshape(queries, grad_slice.shape[1], pieces.shape[0])
    return jnp.einsum("qrt,tr->tq", inner, grad_slice.astype(jnp.float32))


def body(query_grads, out_grads, activations, seq_ids):
    queries, rows_here, cols_here = query_grads.shape
    flat_grads = query_grads.reshape(queries * rows_here, cols_here)
    all_grads = lax.all_gather(out_grads, "col", axis=0, tiled=True)
    all_acts = lax.all_gather(activations, "row", axis=0, tiled=True)
    partial_scores = block_scores(flat_grads, all_acts, all_grads, queries)
    col_summed = lax.psum(partial_scores, "col")
    scores = lax.psum_scatter(col_summed, "row", scatter_dimension=0, tiled=True)
    total_tokens = seq_ids.shape[0] * lax.axis_size("row")
    seq_count = max(total_tokens // 32, 4)
    onehot = (seq_ids[:, None] == jnp.arange(seq_count, dtype=jnp.int32)[None, :]).astype(
        jnp.float32
    )
    local_seq = jnp.dot(onehot.T, scores, precision=lax.Precision.HIGHEST)
    seq_scores = lax.psum(local_seq, "row")
    return (scores, seq_scores)


def solution(mesh):
    placed = (P(None, "row", "col"), P("col", "row"), P("row", "col"), P("row"))
    return jax.shard_map(
        body, mesh=mesh, in_specs=placed, out_specs=(P("row", None), P()), check_vma=False
    )
```

profile of v0, /device:TPU:1, one launch (start us, length us, event | category | flops | bytes accessed | tf_op | source)
XLA Modules:
  0.0 402.5 jit_solution(6016021218678429364)
XLA Ops:
  7.2 0.0 all-gather.2.cloned.1.call-start
  7.2 0.7 all-gather.2.cloned.1.call-update
  7.9 0.0 reduce-scatter.4.cloned.1.call-start
  7.9 11.5 %all_gather.7 = bf16[1024,128]{1,0:T(8,128)(2,1)S(1)} all-gather(bf16[256,128]{1,0:T(8,128)(2,1)} %param.5), channel_id=1, replica_groups=mesh['row'=64,'col'=4] {'col'}, dimensions={0}, use_global_device_ids=true | all-gather | bytes 327680 | tf_op jit(solution)/shard_map/all_gather | solution.py:16
  19.4 0.1 copy.14
  19.6 0.0 copy-start.1
  19.6 90.0 %all-gather.2.cloned.1.call-done = bf16[1024,7168]{1,0:T(8,128)(2,1)} async-done(((bf16[16,7168]{1,0:T(8,128)(2,1)}), bf16[1024,7168]{1,0:T(8,128)(2,1)}) %all-gather.2.cloned.1.call-update) | async-done | bytes 14680080 | tf_op jit(solution)/shard_map/all_gather | solution.py:17
  109.6 13.2 %multiply_reduce_fusion = f32[1024,4]{0,1:T(4,128)S(1)} fusion(bf16[4,128,7168]{2,1,0:T(8,128)(2,1)} %param.4, bf16[1024,7168]{1,0:T(8,128)(2,1)} %all-gather.2.cloned.1.call-done, f32[1024,128]{0,1:T(8,128)S(1)} %copy.14), kind=kOutput, calls=%fused_computation.2 | convolution fusion | flops 7517237248 | bytes 22560768 | tf_op jit(solution)/shard_map/dot_general | solution.py:8
  122.8 1.0 copy.12
  123.8 0.0 reduce-scatter.4.cloned.1.call-update
  123.9 130.7 %reduce-scatter.4.cloned.1.call-done = f32[16,4]{1,0:T(8,128)} async-done(((f32[1024,4]{1,0:T(8,128)}), f32[16,4]{1,0:T(8,128)}) %reduce-scatter.4.cloned.1.call-update) | async-done | bytes 272
  254.5 0.8 copy.13
  255.3 8.4 %psum.16 = f32[16,4]{0,1:T(4,128)S(1)} all-reduce(f32[16,4]{0,1:T(4,128)S(1)} %copy.13), channel_id=1, replica_groups=mesh['row'=64,'col'=4] {'col'}, use_global_device_ids=true, to_apply=%region_0.0 | all-reduce | flops 64 | bytes 512 | tf_op jit(solution)/shard_map/psum | solution.py:19
  263.7 0.0 copy-done.1
  263.7 0.0 copy-start
  263.7 0.2 fusion.4
  263.9 131.7 %psum.15 = f32[32,4]{0,1:T(4,128)} all-reduce(f32[32,4]{0,1:T(4,128)S(1)} %fusion.4), channel_id=1, replica_groups=mesh['row'=64,'col'=4] {'row'}, use_global_device_ids=true, to_apply=%region_2.0 | all-reduce | flops 128 | bytes 1024 | tf_op jit(solution)/shard_map/psum | solution.py:27
  395.6 0.0 copy-done
Async XLA Ops:
  7.2 102.4 %all-gather.2.cloned.1.call-start = ((), (), s32[]{:S(2)}) async-start(), calls=%async_computation.1 | async-start | bytes 14909440 | tf_op jit(solution)/shard_map/all_gather | solution.py:17
  7.9 246.6 %reduce-scatter.4.cloned.1.call-start = ((), (), s32[]{:S(2)}) async-start(), calls=%async_computation.2 | async-start | bytes 532480
  19.6 244.1 %copy-start.1 = (s32[16]{0:T(128)S(1)}, s32[16]{0:T(128)}, u32[]{:S(2)}) copy-start(s32[16]{0:T(128)} %param.7) | copy-start | bytes 196
  263.7 131.9 %copy-start = (f32[16,4]{0,1:T(4,128)}, f32[16,4]{0,1:T(4,128)S(1)}, u32[]{:S(2)}) copy-start(f32[16,4]{0,1:T(4,128)S(1)} %psum.16) | copy-start | bytes 772
Sparse Core Ops, SparseCore 0:
  10.7 98.8 all-gather.1
  124.0 130.5 reduce-scatter.3
where the time goes:
time: 403 us; the launch traced here: 402 us
  waiting for transfers between devices  221 us (55%)
  blocking collectives  152 us (38%)
  between operations  14.1 us (3%)
  matrix products  13.4 us (3%)
    psum x1, blocking collectives, body(): seq_scores = lax.psum(local_seq, 'row')  132 us
    unnamed x3, waiting for transfers between devices  131 us
    all_gather x1, waiting for transfers between devices, body(): all_acts = lax.all_gather(activations, 'row', axis=0, tiled=True)  90 us
    dot_general x1, matrix products, block_scores(): inner = jnp.dot(flat_grads, pieces.T, preferred_element_type=jnp.float32)  13.2 us
    all_gather x1, blocking collectives, body(): all_grads = lax.all_gather(out_grads, 'col', axis=0, tiled=True)  11.5 us
    psum x1, blocking collectives, body(): col_summed = lax.psum(partial_scores, 'col')  8.4 us
  transfers between devices with their start and end apart: 2, of which 2 were waited for; matrix products, arithmetic and copies ran while one was open for 0% of the time, Pallas kernels for 0%

commit v1 on v0

v1 whole, which is shorter than its diff:
```python
import jax
import jax.numpy as jnp
from jax import lax
from jax.sharding import PartitionSpec as P

EXACT = lax.Precision.HIGHEST


def block_scores(flat_grads, pieces, grad_slice, queries):
    inner = jnp.dot(flat_grads, pieces.T, preferred_element_type=jnp.float32)
    inner = inner.reshape(queries, grad_slice.shape[1], pieces.shape[0])
    return jnp.einsum("qrt,tr->qt", inner, grad_slice.astype(jnp.float32))


def body(query_grads, out_grads, activations, seq_ids):
    queries, rows_here, cols_here = query_grads.shape
    rows, cols = lax.axis_size("row"), lax.axis_size("col")
    tokens_here = seq_ids.shape[0]
    flat_grads = query_grads.reshape(queries * rows_here, cols_here)
    all_acts = lax.all_gather(activations, "row", axis=0, tiled=True)
    all_grads = lax.all_gather(out_grads, "col", axis=0, tiled=True)
    copies = jnp.broadcast_to(seq_ids[None, :], (rows, tokens_here))
    all_ids = lax.all_to_all(copies, "row", 0, 0, tiled=True).reshape(-1)
    total_tokens = tokens_here * rows
    seq_count = max(total_tokens // 32, 4)
    onehot = (all_ids[:, None] == jnp.arange(seq_count, dtype=jnp.int32)[None, :]).astype(
        jnp.float32
    )
    partial = block_scores(flat_grads, all_acts, all_grads, queries)
    partial_seq = jnp.dot(partial, onehot, precision=EXACT)
    mine = partial.reshape(queries, rows, tokens_here).transpose(1, 0, 2).reshape(rows, -1)
    parts = jnp.concatenate(
        [mine, jnp.broadcast_to(partial_seq.reshape(1, -1), (rows, queries * seq_count))], axis=1
    )
    parts = jnp.broadcast_to(parts[:, None, :], (rows, cols, parts.shape[1]))
    parts = parts.reshape(rows * cols, -1)
    arrived = lax.all_to_all(parts, ("row", "col"), 0, 0, tiled=True)
    total = jnp.sum(arrived, axis=0)
    split = queries * tokens_here
    scores = total[:split].reshape(queries, tokens_here).T
    seq_scores = total[split:].reshape(queries, seq_count).T
    return (scores, seq_scores)


def solution(mesh):
    placed = (P(None, "row", "col"), P("col", "row"), P("row", "col"), P("row"))
    return jax.shard_map(
        body, mesh=mesh, in_specs=placed, out_specs=(P("row", None), P()), check_vma=False
    )
```

time: 403 us -> 157 us (0.39)
  waiting for transfers between devices: 221 us -> 75.5 us
  blocking collectives: 152 us -> 35.1 us
  starting transfers between devices: 0.08 us -> 13 us
    psum x2 -> x0, blocking collectives: 140 us -> none  [the longest x1 132 us: body(): seq_scores = lax.psum(local_seq, 'row')]
    unnamed x3 -> x1, waiting for transfers between devices: 131 us -> 0.68 us
    all_to_all x0 -> x1, blocking collectives: none -> 24 us  [body(): arrived = lax.all_to_all(parts, ('row', 'col'), 0, 0, tiled=True)]
    all_gather x1, waiting for transfers between devices: 90 us -> 74.8 us  [body(): all_acts = lax.all_gather(activations, 'row', axis=0, tiled=True)]
    all_to_all x0 -> x1, starting transfers between devices: none -> 13 us  [body(): all_ids = lax.all_to_all(copies, 'row', 0, 0, tiled=True).reshape(-1)]
  transfers between devices with their start and end apart: 2 -> 2, of which waited for: 2 -> 1; matrix products, arithmetic and copies ran while one was open for 0% -> 2% of each run, Pallas kernels for 0% -> 0%
where the time goes in v1:
time: 157 us
  waiting for transfers between devices  75.5 us (48%)
  blocking collectives  35.1 us (22%)
  between operations  14.1 us (9%)
  matrix products  13.6 us (9%)
  starting transfers between devices  13 us (8%)
  local copies, waits for them, and re-layouts  4.25 us (3%)
    all_gather x1, waiting for transfers between devices, body(): all_acts = lax.all_gather(activations, 'row', axis=0, tiled=True)  74.8 us
    all_to_all x1, blocking collectives, body(): arrived = lax.all_to_all(parts, ('row', 'col'), 0, 0, tiled=True)  24 us
    dot_general x1, matrix products, block_scores(): inner = jnp.dot(flat_grads, pieces.T, preferred_element_type=jnp.float32)  13.2 us
    all_to_all x1, starting transfers between devices, body(): all_ids = lax.all_to_all(copies, 'row', 0, 0, tiled=True).reshape(-1)  13 us
    all_gather x1, blocking collectives, body(): all_grads = lax.all_gather(out_grads, 'col', axis=0, tiled=True)  11.1 us
  transfers between devices with their start and end apart: 2, of which 1 were waited for; matrix products, arithmetic and copies ran while one was open for 2% of the time, Pallas kernels for 0%

profile of v1, /device:TPU:1, one launch (start us, length us, event | category | flops | bytes accessed | tf_op | source)
XLA Modules:
  0.0 156.6 jit_solution(11412013479772242063)
XLA Ops:
  7.2 0.0 all-gather.2.cloned.1.call-start
  7.2 0.7 all-gather.2.cloned.1.call-update
  7.9 1.3 broadcast_in_dim.8
  9.2 13.0 %all-to-all-start = ((s32[64,1,16]{2,1,0:T(1,128)}), s32[64,1,16]{2,1,0:T(1,128)S(1)}, u32[]{:S(2)}, u32[]{:S(2)}) async-start(s32[64,1,16]{2,1,0:T(1,128)} %broadcast_in_dim.8), calls=%async_computation | async-start | bytes 65536 | tf_op jit(solution)/shard_map/all_to_all | solution.py:23
  22.2 11.1 %all_gather.7 = bf16[1024,128]{1,0:T(8,128)(2,1)S(1)} all-gather(bf16[256,128]{1,0:T(8,128)(2,1)} %param.5), channel_id=1, replica_groups=mesh['row'=64,'col'=4] {'col'}, dimensions={0}, use_global_device_ids=true | all-gather | bytes 327680 | tf_op jit(solution)/shard_map/all_gather | solution.py:21
  33.3 0.1 copy.18
  33.5 0.0 all-to-all-done
  33.5 0.5 broadcast.10
  34.0 0.7 reduce.6
  34.7 0.1 eq.15
  34.8 74.8 %all-gather.2.cloned.1.call-done = bf16[1024,7168]{1,0:T(8,128)(2,1)} async-done(((bf16[16,7168]{1,0:T(8,128)(2,1)}), bf16[1024,7168]{1,0:T(8,128)(2,1)}) %all-gather.2.cloned.1.call-update) | async-done | bytes 14680080 | tf_op jit(solution)/shard_map/all_gather | solution.py:20
  109.6 13.2 %multiply_reduce_fusion = f32[1024,4]{0,1:T(4,128)S(1)} fusion(bf16[4,128,7168]{2,1,0:T(8,128)(2,1)} %param.4, bf16[1024,7168]{1,0:T(8,128)(2,1)} %all-gather.2.cloned.1.call-done, f32[1024,128]{0,1:T(8,128)S(1)} %copy.18), kind=kOutput, calls=%fused_computation.2 | convolution fusion | flops 7517237248 | bytes 22560768 | tf_op jit(solution)/shard_map/dot_general | solution.py:10
  122.8 0.1 reshape.51
  122.9 0.1 copy.9
  123.0 0.1 copy.10
  123.1 0.4 fusion.4
  123.5 0.1 reshape.64
  123.5 0.1 pad.1.clone
  123.6 0.1 broadcast_in_dim.11
  123.7 0.4 all_to_all.13
  124.1 24.0 %all_to_all.16 = f32[256,1,192]{2,1,0:T(1,128)S(1)} all-to-all(f32[256,1,192]{2,1,0:T(1,128)S(1)} %all_to_all.13), channel_id=1, replica_groups=mesh['row'=64,'col'=4] {'row','col'}, dimensions={0} | all-to-all | bytes 393216 | tf_op jit(solution)/shard_map/all_to_all | solution.py:37
  148.1 0.3 reduce_sum.9
  148.4 0.1 slice.23
  148.5 0.7 reshape.53
  149.1 0.7 reshape.54
  (2 shorter events, 0.0 us)
Async XLA Ops:
  7.2 102.4 %all-gather.2.cloned.1.call-start = ((), (), s32[]{:S(2)}) async-start(), calls=%async_computation.2 | async-start | bytes 14909440 | tf_op jit(solution)/shard_map/all_gather | solution.py:20
  9.2 24.3 %all-to-all-start = ((s32[64,1,16]{2,1,0:T(1,128)}), s32[64,1,16]{2,1,0:T(1,128)S(1)}, u32[]{:S(2)}, u32[]{:S(2)}) async-start(s32[64,1,16]{2,1,0:T(1,128)} %broadcast_in_dim.8), calls=%async_computation | async-start | bytes 65536 | tf_op jit(solution)/shard_map/all_to_all | solution.py:23
Sparse Core Ops, SparseCore 0:
  10.7 98.8 all-gather.1

commit v2 on v1

v2 whole, which is shorter than its diff:
```python
import jax
import jax.numpy as jnp
import numpy as np
from jax import lax
from jax.sharding import PartitionSpec as P

EXACT = lax.Precision.HIGHEST
NX, NZ = 4, 8


def cat(parts, axis=0):
    return parts[0] if len(parts) == 1 else jnp.concatenate(parts, axis)


def shift(block, dx, dz):
    pairs = [
        ((x * NZ + z) * 2 + c, ((x + dx) % NX * NZ + (z + dz) % NZ) * 2 + c)
        for x in range(NX)
        for z in range(NZ)
        for c in range(2)
    ]
    return lax.ppermute(block, "row", pairs)


def swap(block):
    return lax.ppermute(block, "row", [(i, i ^ 1) for i in range(NX * NZ * 2)])


def from_col(block, ahead, cols):
    return lax.ppermute(block, "col", [(i, (i - ahead) % cols) for i in range(cols)])


L, H, F = (0,), (1,), (0, 1)
E = (1, 0), (-1, 0), (0, 1), (0, -1)
ROUNDS = [
    [(d, [((0, 0), F, d)]) for d in E],
    [
        (E[0], [((1, 0), L, (2, 0)), ((0, 1), F, (1, 1))]),
        (E[1], [((-1, 0), H, (2, 0)), ((0, -1), F, (-1, -1))]),
        (E[2], [((0, 1), F, (0, 2)), ((-1, 0), F, (-1, 1))]),
        (E[3], [((0, -1), F, (0, -2)), ((1, 0), F, (1, -1))]),
    ],
    [
        (E[0], [((1, 1), L, (2, 1)), ((1, -1), L, (2, -1)), ((0, 2), F, (1, 2))]),
        (E[1], [((-1, 1), H, (2, 1)), ((-1, -1), H, (2, -1)), ((0, -2), F, (-1, -2))]),
        (E[2], [((0, 2), F, (0, 3)), ((-1, 1), F, (-1, 2))]),
        (E[3], [((0, -2), F, (0, -3)), ((1, -1), F, (1, -2))]),
    ],
    [
        (E[0], [((1, 2), L, (2, 2)), ((1, -2), L, (2, -2)), ((0, 3), F, (1, 3))]),
        (E[1], [((-1, 2), H, (2, 2)), ((-1, -2), H, (2, -2)), ((0, -3), F, (-1, -3))]),
        (E[2], [((0, 3), L, (0, 4)), ((-1, 2), F, (-1, 3))]),
        (E[3], [((0, -3), H, (0, 4)), ((1, -2), F, (1, -3))]),
    ],
    [
        (E[0], [((1, 3), L, (2, 3)), ((1, -3), L, (2, -3))]),
        (E[1], [((-1, 3), H, (2, 3)), ((-1, -3), H, (2, -3))]),
        (E[2], [((1, 3), L, (1, 4)), ((-1, 3), L, (-1, 4))]),
        (E[3], [((1, -3), H, (1, 4)), ((-1, -3), H, (-1, 4))]),
        ((1, 1), [((1, 3), F, (2, 4))]),
    ],
]


def body(query_grads, out_grads, activations, seq_ids):
    queries, rows_here, width = query_grads.shape
    half = width // 2
    tokens = seq_ids.shape[0]
    rows, cols = lax.axis_size("row"), lax.axis_size("col")
    seq_count = max(tokens * rows // 32, 4)
    row, y = lax.axis_index("row"), lax.axis_index("col")
    core, z, x = row % 2, row // 2 % NZ, row // (2 * NZ)

    def columns(array, which):
        start = (0,) * (array.ndim - 1) + (which * half,)
        return lax.dynamic_slice(array, start, array.shape[:-1] + (half,))

    ids = jnp.broadcast_to(seq_ids[:, None].astype(activations.dtype), (tokens, 128))
    mine = cat([columns(activations, core), ids], 1)
    other = swap(cat([columns(activations, 1 - core), ids], 1))
    own = jnp.where(core == 0, cat([mine, other]), cat([other, mine]))

    grads = cat([columns(query_grads, core), swap(columns(query_grads, 1 - core))])
    grads = grads.reshape(2 * queries * rows_here, half)
    slices = cat([out_grads, swap(out_grads)], 1)
    slices = jnp.stack([slices] + [from_col(slices, k, cols) for k in range(1, cols)])
    slices = lax.dynamic_slice_in_dim(cat([slices, slices]), (x - y) % NX, NX)
    slices = slices.reshape(NX, NZ, 2, tokens, 2 * rows_here)
    slices = lax.dynamic_slice_in_dim(cat([slices, slices], 1), z, NZ, 1)

    held = {((0, 0), h): own[h * tokens : (h + 1) * tokens] for h in F}
    slots, scores, came_ids = [], [], []

    def work(arrays, places):
        block = cat(arrays)
        weights = cat([slices[-ox % NX, -oz % NZ, h] for (ox, oz), h in places])
        inner = lax.dot_general(
            grads, block[:, :half], (((1,), (1,)), ((), ())), preferred_element_type=jnp.float32
        )
        inner = inner.reshape(2, queries, rows_here, block.shape[0])
        weights = weights.astype(jnp.float32).T.reshape(2, 1, rows_here, block.shape[0])
        scores.append(jnp.sum(inner * weights, axis=(0, 2)))
        came_ids.append(block[:, half])
        slots.extend(places)

    arrays, places = [own], [((0, 0), h) for h in F]
    for moves in ROUNDS:
        came = []
        for (dx, dz), load in moves:
            sent = cat([cat([held[src, h] for h in part]) for src, part, _ in load])
            came.append((shift(sent, dx, dz), [(dst, h) for _, part, dst in load for h in part]))
        for array, names in came:
            for i, name in enumerate(names):
                held[name] = array[i * tokens : (i + 1) * tokens]
            arrays.append(array)
            places += names
        work(arrays, places)
        arrays, places = [], []

    partial = cat(scores, 1)
    all_ids = cat(came_ids).astype(jnp.int32)
    onehot = all_ids[:, None] == jnp.arange(seq_count, dtype=jnp.int32)[None, :]
    partial_seq = jnp.dot(partial, onehot.astype(jnp.float32), precision=EXACT)
    far = np.array([(NX - ox, NZ - oz, h) for (ox, oz), h in slots], np.int32).T
    owner = ((x + far[0]) % NX * NZ + (z + far[1]) % NZ) * 2 + far[2]
    place = owner[:, None] == jnp.arange(rows, dtype=jnp.int32)[None, :]
    mine = jnp.einsum(
        "qst,so->oqt",
        partial.reshape(queries, rows, tokens),
        place.astype(jnp.float32),
        precision=EXACT,
    ).reshape(rows, -1)
    parts = cat(
        [mine, jnp.broadcast_to(partial_seq.reshape(1, -1), (rows, queries * seq_count))], 1
    )
    parts = jnp.broadcast_to(parts[:, None, :], (rows, cols, parts.shape[1]))
    parts = parts.reshape(rows * cols, -1)
    arrived = lax.all_to_all(parts, ("row", "col"), 0, 0, tiled=True)
    total = jnp.sum(arrived, axis=0)
    split = queries * tokens
    scores = total[:split].reshape(queries, tokens).T
    seq_scores = total[split:].reshape(queries, seq_count).T
    return (scores, seq_scores)


def solution(mesh):
    placed = (P(None, "row", "col"), P("col", "row"), P("row", "col"), P("row"))
    return jax.shard_map(
        body, mesh=mesh, in_specs=placed, out_specs=(P("row", None), P()), check_vma=False
    )
```

time: 157 us -> 156 us (level)
  waiting for transfers between devices: 75.5 us -> 38.8 us
  starting transfers between devices: 13 us -> 40.9 us
  local copies, waits for them, and re-layouts: 4.25 us -> 19.7 us
  between operations: 14.1 us -> 1.55 us
  other arithmetic: 1.03 us -> 8.54 us
  blocking collectives: 35.1 us -> 29.7 us
  matrix products: 13.6 us -> 16.3 us
    all_gather x1 -> x0, waiting for transfers between devices: 74.8 us -> none  [body(): all_acts = lax.all_gather(activations, 'row', axis=0, tiled=True)]
    ppermute x0 -> x27, starting transfers between devices: none -> 40.9 us  [the longest x21 35 us: shift(): return lax.ppermute(block, 'row', pairs)]
    ppermute x0 -> x27, waiting for transfers between devices: none -> 38.8 us  [the longest x21 32.3 us: shift(): return lax.ppermute(block, 'row', pairs)]
    all_to_all x1 -> x0, starting transfers between devices: 13 us -> none  [body(): all_ids = lax.all_to_all(copies, 'row', 0, 0, tiled=True).reshape(-1)]
    all_gather x1 -> x0, blocking collectives: 11.1 us -> none  [body(): all_grads = lax.all_gather(out_grads, 'col', axis=0, tiled=True)]
    unnamed x1 -> x73, local copies, waits for them, and re-layouts: 0.14 us -> 8.56 us
    concatenate x1 -> x15, other arithmetic: 0.01 us -> 7.41 us  [cat(): return parts[0] if len(parts) == 1 else jnp.concatenate(parts, axis)]
    dynamic_slice x0 -> x3, local copies, waits for them, and re-layouts: none -> 6.79 us  [the longest x2 6.74 us: columns(): return lax.dynamic_slice(array, start, array.shape[:-1] + (half,))]
  transfers between devices with their start and end apart: 2 -> 27, of which waited for: 1 -> 11; matrix products, arithmetic and copies ran while one was open for 2% -> 7% of each run, Pallas kernels for 0% -> 0%
where the time goes in v2:
time: 156 us; the launch traced here: 155 us
  starting transfers between devices  40.9 us (26%)
  waiting for transfers between devices  38.8 us (25%)
  blocking collectives  29.7 us (19%)
  local copies, waits for them, and re-layouts  19.7 us (13%)
  matrix products  16.3 us (10%)
  other arithmetic  8.54 us (5%)
    ppermute x21, starting transfers between devices, shift(): return lax.ppermute(block, 'row', pairs)  35 us
    ppermute x21, waiting for transfers between devices, shift(): return lax.ppermute(block, 'row', pairs)  32.3 us
    all_to_all x1, blocking collectives, body(): arrived = lax.all_to_all(parts, ('row', 'col'), 0, 0, tiled=True)  29.7 us
    dot_general x5, matrix products, work(): lax.dot_general(grads, block[:, :half], (((1,), (1,)), ((), ())), preferr...  15.6 us
    unnamed x73, local copies, waits for them, and re-layouts  8.56 us
    concatenate x15, other arithmetic, cat(): return parts[0] if len(parts) == 1 else jnp.concatenate(parts, axis)  7.41 us
    dynamic_slice x2, local copies, waits for them, and re-layouts, columns(): return lax.dynamic_slice(array, start, array.shape[:-1] + (half,))  6.74 us
    ppermute x3, waiting for transfers between devices, swap(): return lax.ppermute(block, 'row', [(i, i ^ 1) for i in range(NX * NZ * 2)])  5.39 us
  transfers between devices with their start and end apart: 27, of which 11 were waited for; matrix products, arithmetic and copies ran while one was open for 7% of the time, Pallas kernels for 0%

profile of v2, /device:TPU:1, one launch (start us, length us, event | category | flops | bytes accessed | tf_op | source)
XLA Modules:
  0.0 155.4 jit_solution(16586221509158736813)
XLA Ops:
  0.7 6.7 %constant_dynamic-slice_fusion.4 = (bf16[4,128,3584]{2,1,0:T(8,128)(2,1)}, bf16[4,128,3584]{2,1,0:T(8,128)(2,1)}) fusion(bf16[4,128,7168]{2,1,0:T(8,128)(2,1)} %param.7, s32[]{:T(128)S(6)} %select_n.60, s32[]{:T(128)S(6)} %select_n.61), kind=kLoop, calls=%fused_computation.229 | loop fusion | bytes 14680072 | tf_op jit(solution)/shard_map/dynamic_slice | solution.py:76
  7.4 3.2 %collective-permute-start = (bf16[4,128,3584]{2,1,0:T(8,128)(2,1)}, bf16[4,128,3584]{2,1,0:T(8,128)(2,1)}, u32[]{:S(2)}, u32[]{:S(2)}) collective-permute-start(bf16[4,128,3584]{2,1,0:T(8,128)(2,1)} %get-tuple-element.3), channel_id=1, source_target_pairs={{0,4},{4,0},{8,12},{12,8},{16,20},{20,16},{24,28},{28,24},{32,36},... | collective-permute-start | bytes 11010056 | tf_op jit(solution)/shard_map/ppermute | solution.py:26
  10.9 0.5 collective-permute-start.6
  11.5 5.4 %collective-permute-done.6 = bf16[256,128]{1,0:T(8,128)(2,1)S(1)} collective-permute-done((bf16[256,128]{1,0:T(8,128)(2,1)S(1)}, bf16[256,128]{1,0:T(8,128)(2,1)S(1)}, u32[]{:S(2)}, u32[]{:S(2)}) %collective-permute-start.6) | collective-permute-done | bytes 65568 | tf_op jit(solution)/shard_map/ppermute | solution.py:26
  16.9 1.1 collective-permute-start.7
  18.3 0.7 collective-permute-start.9
  19.0 0.7 maximum_select_fusion
  19.7 1.2 collective-permute-start.2
  21.0 1.0 collective-permute-done.7
  21.9 3.9 %collective-permute-start.3 = (bf16[32,3712]{1,0:T(8,128)(2,1)S(1)}, bf16[32,3712]{1,0:T(8,128)(2,1)S(1)}, u32[]{:S(2)}, u32[]{:S(2)}) collective-permute-start(bf16[32,3712]{1,0:T(8,128)(2,1)S(1)} %get-tuple-element.74), channel_id=1, source_target_pairs={{0,192},{4,196},{8,200},{12,204},{16,208},{20,212},{24,216},{28,22... | collective-permute-start | bytes 712712 | tf_op jit(solution)/shard_map/ppermute | solution.py:22
  25.9 1.7 %collective-permute-start.4 = (bf16[32,3712]{1,0:T(8,128)(2,1)S(1)}, bf16[32,3712]{1,0:T(8,128)(2,1)S(1)}, u32[]{:S(2)}, u32[]{:S(2)}) collective-permute-start(bf16[32,3712]{1,0:T(8,128)(2,1)S(1)} %get-tuple-element.74), channel_id=1, source_target_pairs={{0,8},{4,12},{8,16},{12,20},{16,24},{20,28},{24,32},{28,36},{32,40... | collective-permute-start | bytes 712712 | tf_op jit(solution)/shard_map/ppermute | solution.py:22
  27.7 5.6 %collective-permute-start.5 = (bf16[32,3712]{1,0:T(8,128)(2,1)S(1)}, bf16[32,3712]{1,0:T(8,128)(2,1)S(1)}, u32[]{:S(2)}, u32[]{:S(2)}) collective-permute-start(bf16[32,3712]{1,0:T(8,128)(2,1)S(1)} %get-tuple-element.74), channel_id=1, source_target_pairs={{0,56},{4,60},{8,0},{12,4},{16,8},{20,12},{24,16},{28,20},{32,24},... | collective-permute-start | bytes 712712 | tf_op jit(solution)/shard_map/ppermute | solution.py:22
  33.7 0.7 copy-done.1
  34.4 0.8 constant_dynamic-update-slice_fusion.94
  35.2 0.8 constant_dynamic-update-slice_fusion.93
  36.0 0.8 constant_dynamic-update-slice_fusion.92
  36.7 0.8 constant_dynamic-update-slice_fusion.91
  37.5 0.8 constant_dynamic-update-slice_fusion.90
  38.3 0.8 constant_dynamic-update-slice_fusion.89
  39.0 0.8 constant_dynamic-update-slice_fusion.88
  39.8 0.8 constant_dynamic-update-slice_fusion.87
  40.6 0.8 constant_dynamic-update-slice_fusion.86
  41.7 1.3 collective-permute-start.10
  43.0 1.5 collective-permute-start.11
  44.8 2.7 %collective-permute-start.13 = (bf16[64,3712]{1,0:T(8,128)(2,1)S(1)}, bf16[64,3712]{1,0:T(8,128)(2,1)S(1)}, u32[]{:S(2)}, u32[]{:S(2)}) collective-permute-start(bf16[64,3712]{1,0:T(8,128)(2,1)S(1)} %pad_maximum_fusion.2), channel_id=1, source_target_pairs={{0,56},{4,60},{8,0},{12,4},{16,8},{20,12},{24,16},{28,20},{32,24},... | collective-permute-start | bytes 1425416 | tf_op jit(solution)/shard_map/ppermute | solution.py:22
  47.7 4.3 %collective-permute-done.10 = bf16[48,3712]{1,0:T(8,128)(2,1)S(1)} collective-permute-done((bf16[48,3712]{1,0:T(8,128)(2,1)S(1)}, bf16[48,3712]{1,0:T(8,128)(2,1)S(1)}, u32[]{:S(2)}, u32[]{:S(2)}) %collective-permute-start.10) | collective-permute-done | bytes 356384 | tf_op jit(solution)/shard_map/ppermute | solution.py:22
  52.2 4.8 %collective-permute-done.12 = bf16[64,3712]{1,0:T(8,128)(2,1)S(1)} collective-permute-done((bf16[64,3712]{1,0:T(8,128)(2,1)S(1)}, bf16[64,3712]{1,0:T(8,128)(2,1)S(1)}, u32[]{:S(2)}, u32[]{:S(2)}) %collective-permute-start.12) | collective-permute-done | bytes 475168 | tf_op jit(solution)/shard_map/ppermute | solution.py:22
  57.4 2.7 %collective-permute-start.15 = (bf16[64,3712]{1,0:T(8,128)(2,1)S(1)}, bf16[64,3712]{1,0:T(8,128)(2,1)S(1)}, u32[]{:S(2)}, u32[]{:S(2)}) collective-permute-start(bf16[64,3712]{1,0:T(8,128)(2,1)S(1)} %pad_maximum_fusion.4), channel_id=1, source_target_pairs={{0,192},{4,196},{8,200},{12,204},{16,208},{20,212},{24,216},{28,22... | collective-permute-start | bytes 1425416 | tf_op jit(solution)/shard_map/ppermute | solution.py:22
  60.1 2.7 %collective-permute-start.17 = (bf16[64,3712]{1,0:T(8,128)(2,1)S(1)}, bf16[64,3712]{1,0:T(8,128)(2,1)S(1)}, u32[]{:S(2)}, u32[]{:S(2)}) collective-permute-start(bf16[64,3712]{1,0:T(8,128)(2,1)S(1)} %collective-permute-done.13), channel_id=1, source_target_pairs={{0,56},{4,60},{8,0},{12,4},{16,8},{20,12},{24,16},{28,20},{32,24},... | collective-permute-start | bytes 1425416 | tf_op jit(solution)/shard_map/ppermute | solution.py:22
  63.0 6.9 %collective-permute-done.17 = bf16[64,3712]{1,0:T(8,128)(2,1)S(1)} collective-permute-done((bf16[64,3712]{1,0:T(8,128)(2,1)S(1)}, bf16[64,3712]{1,0:T(8,128)(2,1)S(1)}, u32[]{:S(2)}, u32[]{:S(2)}) %collective-permute-start.17) | collective-permute-done | bytes 475168 | tf_op jit(solution)/shard_map/ppermute | solution.py:22
  69.9 1.0 collective-permute-done.16
  71.2 2.7 %collective-permute-start.19 = (bf16[64,3712]{1,0:T(8,128)(2,1)S(1)}, bf16[64,3712]{1,0:T(8,128)(2,1)S(1)}, u32[]{:S(2)}, u32[]{:S(2)}) collective-permute-start(bf16[64,3712]{1,0:T(8,128)(2,1)S(1)} %pad_maximum_fusion.6), channel_id=1, source_target_pairs={{0,192},{4,196},{8,200},{12,204},{16,208},{20,212},{24,216},{28,22... | collective-permute-start | bytes 1425416 | tf_op jit(solution)/shard_map/ppermute | solution.py:22
  74.1 2.7 %collective-permute-start.21 = (bf16[48,3712]{1,0:T(8,128)(2,1)S(1)}, bf16[48,3712]{1,0:T(8,128)(2,1)S(1)}, u32[]{:S(2)}, u32[]{:S(2)}) collective-permute-start(bf16[48,3712]{1,0:T(8,128)(2,1)S(1)} %slice.501), channel_id=1, source_target_pairs={{0,56},{4,60},{8,0},{12,4},{16,8},{20,12},{24,16},{28,20},{32,24},... | collective-permute-start | bytes 1069064 | tf_op jit(solution)/shard_map/ppermute | solution.py:22
  77.2 4.7 %collective-permute-done.20 = bf16[48,3712]{1,0:T(8,128)(2,1)S(1)} collective-permute-done((bf16[48,3712]{1,0:T(8,128)(2,1)S(1)}, bf16[48,3712]{1,0:T(8,128)(2,1)S(1)}, u32[]{:S(2)}, u32[]{:S(2)}) %collective-permute-start.20) | collective-permute-done | bytes 356384 | tf_op jit(solution)/shard_map/ppermute | solution.py:22
  82.1 2.7 %collective-permute-start.23 = (bf16[32,3712]{1,0:T(8,128)(2,1)S(1)}, bf16[32,3712]{1,0:T(8,128)(2,1)S(1)}, u32[]{:S(2)}, u32[]{:S(2)}) collective-permute-start(bf16[32,3712]{1,0:T(8,128)(2,1)S(1)} %get-tuple-element.79), channel_id=1, source_target_pairs={{0,192},{4,196},{8,200},{12,204},{16,208},{20,212},{24,216},{28,22... | collective-permute-start | bytes 712712 | tf_op jit(solution)/shard_map/ppermute | solution.py:22
  84.9 2.7 %collective-permute-start.25 = (bf16[32,3712]{1,0:T(8,128)(2,1)S(1)}, bf16[32,3712]{1,0:T(8,128)(2,1)S(1)}, u32[]{:S(2)}, u32[]{:S(2)}) collective-permute-start(bf16[32,3712]{1,0:T(8,128)(2,1)S(1)} %get-tuple-element.78), channel_id=1, source_target_pairs={{0,56},{4,60},{8,0},{12,4},{16,8},{20,12},{24,16},{28,20},{32,24},... | collective-permute-start | bytes 712712 | tf_op jit(solution)/shard_map/ppermute | solution.py:22
  88.3 2.8 %collective-permute-done.24 = bf16[32,3712]{1,0:T(8,128)(2,1)S(1)} collective-permute-done((bf16[32,3712]{1,0:T(8,128)(2,1)S(1)}, bf16[32,3712]{1,0:T(8,128)(2,1)S(1)}, u32[]{:S(2)}, u32[]{:S(2)}) %collective-permute-start.24) | collective-permute-done | bytes 237600 | tf_op jit(solution)/shard_map/ppermute | solution.py:22
  91.2 7.6 %collective-permute-done.26 = bf16[32,3712]{1,0:T(8,128)(2,1)S(1)} collective-permute-done((bf16[32,3712]{1,0:T(8,128)(2,1)S(1)}, bf16[32,3712]{1,0:T(8,128)(2,1)S(1)}, u32[]{:S(2)}, u32[]{:S(2)}) %collective-permute-start.26) | collective-permute-done | bytes 237600 | tf_op jit(solution)/shard_map/ppermute | solution.py:22
  98.8 1.0 copy-done.11
  100.0 6.7 %pad_maximum_fusion = bf16[8,128,3584]{2,1,0:T(8,128)(2,1)} fusion(bf16[4,128,3584]{2,1,0:T(8,128)(2,1)} %collective-permute-done, bf16[4,128,3584]{2,1,0:T(8,128)(2,1)} %get-tuple-element.2), kind=kLoop, calls=%fused_computation | loop fusion | flops 3670016 | bytes 14680064 | tf_op jit(solution)/shard_map/concatenate | solution.py:12
  106.8 5.9 %fusion.9 = f32[4,160]{1,0:T(4,128)S(1)} fusion(bf16[2,4,128,3584]{3,2,1,0:T(8,128)(2,1)} %bitcast.345, bf16[160,3712]{1,0:T(8,128)(2,1)S(1)} %constant_dynamic-update-slice_fusion, f32[2,128,160]{1,2,0:T(8,128)S(1)} %copy_bitcast_fusion.3), kind=kOutput, calls=%fused_computation.15 | convolution fusion | flops 1174732160 | bytes 8653312 | tf_op jit(solution)/shard_map/dot_general | solution.py:97
  112.7 2.5 %fusion.8 = f32[4,224]{1,0:T(4,128)S(1)} fusion(bf16[2,4,128,3584]{3,2,1,0:T(8,128)(2,1)S(1)} %bitcast.346, bf16[224,3712]{1,0:T(8,128)(2,1)S(1)} %copy-done.8, f32[2,128,224]{1,2,0:T(8,128)S(1)} %copy_bitcast_fusion.1), kind=kOutput, calls=%fused_computation.14 | convolution fusion | flops 1644625024 | bytes 9178624 | tf_op jit(solution)/shard_map/dot_general | solution.py:97
  115.2 2.1 %fusion.6 = f32[4,256]{1,0:T(4,128)S(1)} fusion(bf16[2,4,128,3584]{3,2,1,0:T(8,128)(2,1)S(1)} %bitcast.347, bf16[256,3712]{1,0:T(8,128)(2,1)S(1)} %copy-done.6, f32[2,128,256]{2,1,0:T(8,128)S(1)} %bitcast.352), kind=kOutput, calls=%fused_computation.12 | convolution fusion | flops 1879571456 | bytes 9441280 | tf_op jit(solution)/shard_map/dot_general | solution.py:97
  117.3 2.4 %fusion.7 = f32[4,224]{1,0:T(4,128)S(1)} fusion(bf16[2,4,128,3584]{3,2,1,0:T(8,128)(2,1)S(1)} %bitcast.348, bf16[224,3712]{1,0:T(8,128)(2,1)S(1)} %copy-done.4, f32[2,128,224]{1,2,0:T(8,128)S(1)} %copy_bitcast_fusion), kind=kOutput, calls=%fused_computation.13 | convolution fusion | flops 1644625024 | bytes 9178624 | tf_op jit(solution)/shard_map/dot_general | solution.py:97
  119.8 2.7 %fusion.10 = f32[4,160]{1,0:T(4,128)S(1)} fusion(bf16[2,4,128,3584]{3,2,1,0:T(8,128)(2,1)S(1)} %bitcast.349, bf16[160,3712]{1,0:T(8,128)(2,1)S(1)} %copy-done.12, f32[2,128,160]{1,2,0:T(8,128)S(1)} %copy_bitcast_fusion.2), kind=kOutput, calls=%fused_computation.16 | convolution fusion | flops 1174732160 | bytes 8653312 | tf_op jit(solution)/shard_map/dot_general | solution.py:97
  124.1 29.7 %all_to_all.10 = f32[256,1,192]{2,1,0:T(1,128)S(1)} all-to-all(f32[256,1,192]{2,1,0:T(1,128)S(1)} %all_to_all.8), channel_id=1, replica_groups=mesh['row'=64,'col'=4] {'row','col'}, dimensions={0} | all-to-all | bytes 393216 | tf_op jit(solution)/shard_map/all_to_all | solution.py:138
  154.1 0.7 reshape.108
  154.8 0.7 reshape.109
  (162 shorter events, 6.2 us)
Async XLA Ops:
  0.7 10.0 %copy-start.16 = (s32[16]{0:T(128)S(1)}, s32[16]{0:T(128)}, u32[]{:S(2)}) copy-start(s32[16]{0:T(128)} %param.10) | copy-start | bytes 196
  0.7 10.0 %copy-start.2 = (bf16[16,7168]{1,0:T(8,128)(2,1)S(1)}, bf16[16,7168]{1,0:T(8,128)(2,1)}, u32[]{:S(2)}) copy-start(bf16[16,7168]{1,0:T(8,128)(2,1)} %param.9) | copy-start | bytes 688132
  0.7 10.2 %copy-start.9 = (bf16[256,128]{1,0:T(8,128)(2,1)S(1)}, bf16[256,128]{1,0:T(8,128)(2,1)}, u32[]{:S(2)}) copy-start(bf16[256,128]{1,0:T(8,128)(2,1)} %param.8) | copy-start | bytes 196612
  0.7 10.7 %copy-start.13 = (s32[64]{0:T(128)S(1)}, s32[64]{0:T(128)}, u32[]{:S(2)}) copy-start(s32[64]{0:T(128)} %constant.95.clone) | copy-start | bytes 772
  0.7 10.7 %copy-start.14 = (s32[64]{0:T(128)S(1)}, s32[64]{0:T(128)}, u32[]{:S(2)}) copy-start(s32[64]{0:T(128)} %constant.94.clone) | copy-start | bytes 772
  0.7 10.7 %copy-start.15 = (s32[64]{0:T(128)S(1)}, s32[64]{0:T(128)}, u32[]{:S(2)}) copy-start(s32[64]{0:T(128)} %constant.93.clone) | copy-start | bytes 772
  7.4 92.6 %collective-permute-start = (bf16[4,128,3584]{2,1,0:T(8,128)(2,1)}, bf16[4,128,3584]{2,1,0:T(8,128)(2,1)}, u32[]{:S(2)}, u32[]{:S(2)}) collective-permute-start(bf16[4,128,3584]{2,1,0:T(8,128)(2,1)} %get-tuple-element.3), channel_id=1, source_target_pairs={{0,4},{4,0},{8,12},{12,8},{16,20},{20,16},{24,28},{28,24},{32,36},... | collective-permute-start | bytes 11010056 | tf_op jit(solution)/shard_map/ppermute | solution.py:26
  10.8 8.2 %collective-permute-start.1 = (bf16[16,3712]{1,0:T(8,128)(2,1)S(1)}, bf16[16,3712]{1,0:T(8,128)(2,1)S(1)}, u32[]{:S(2)}, u32[]{:S(2)}) collective-permute-start(bf16[16,3712]{1,0:T(8,128)(2,1)S(1)} %pad_maximum_fusion.14), channel_id=1, source_target_pairs={{0,4},{4,0},{8,12},{12,8},{16,20},{20,16},{24,28},{28,24},{32,36},... | collective-permute-start | bytes 356360 | tf_op jit(solution)/shard_map/ppermute | solution.py:26
  10.9 5.9 %collective-permute-start.6 = (bf16[256,128]{1,0:T(8,128)(2,1)S(1)}, bf16[256,128]{1,0:T(8,128)(2,1)S(1)}, u32[]{:S(2)}, u32[]{:S(2)}) collective-permute-start(bf16[256,128]{1,0:T(8,128)(2,1)S(1)} %copy-done.9), channel_id=1, source_target_pairs={{0,4},{4,0},{8,12},{12,8},{16,20},{20,16},{24,28},{28,24},{32,36},... | collective-permute-start | bytes 196616 | tf_op jit(solution)/shard_map/ppermute | solution.py:26
  16.9 5.0 %collective-permute-start.7 = (bf16[256,256]{1,0:T(8,128)(2,1)S(1)}, bf16[256,256]{1,0:T(8,128)(2,1)S(1)}, u32[]{:S(2)}, u32[]{:S(2)}) collective-permute-start(bf16[256,256]{1,0:T(8,128)(2,1)S(1)} %constant_dynamic-update-slice_fusion.5), channel_id=1, source_target_pairs={{0,3},{1,0},{2,1},{3,2},{4,7},{5,4},{6,5},{7,6},{8,11},{9,8},{10,9... | collective-permute-start | bytes 393224 | tf_op jit(solution)/shard_map/ppermute | solution.py:30
  17.9 7.9 %collective-permute-start.8 = (bf16[256,256]{1,0:T(8,128)(2,1)S(1)}, bf16[256,256]{1,0:T(8,128)(2,1)S(1)}, u32[]{:S(2)}, u32[]{:S(2)}) collective-permute-start(bf16[256,256]{1,0:T(8,128)(2,1)S(1)} %constant_dynamic-update-slice_fusion.5), channel_id=1, source_target_pairs={{0,2},{1,3},{2,0},{3,1},{4,6},{5,7},{6,4},{7,5},{8,10},{9,11},{10,... | collective-permute-start | bytes 393224 | tf_op jit(solution)/shard_map/ppermute | solution.py:30
  18.3 9.4 %collective-permute-start.9 = (bf16[256,256]{1,0:T(8,128)(2,1)S(1)}, bf16[256,256]{1,0:T(8,128)(2,1)S(1)}, u32[]{:S(2)}, u32[]{:S(2)}) collective-permute-start(bf16[256,256]{1,0:T(8,128)(2,1)S(1)} %constant_dynamic-update-slice_fusion.5), channel_id=1, source_target_pairs={{0,1},{1,2},{2,3},{3,0},{4,5},{5,6},{6,7},{7,4},{8,9},{9,10},{10,1... | collective-permute-start | bytes 393224 | tf_op jit(solution)/shard_map/ppermute | solution.py:30
  19.7 21.9 %collective-permute-start.2 = (bf16[32,3712]{1,0:T(8,128)(2,1)S(1)}, bf16[32,3712]{1,0:T(8,128)(2,1)S(1)}, u32[]{:S(2)}, u32[]{:S(2)}) collective-permute-start(bf16[32,3712]{1,0:T(8,128)(2,1)S(1)} %get-tuple-element.74), channel_id=1, source_target_pairs={{0,64},{4,68},{8,72},{12,76},{16,80},{20,84},{24,88},{28,92},{32,9... | collective-permute-start | bytes 712712 | tf_op jit(solution)/shard_map/ppermute | solution.py:22
  21.9 21.1 %collective-permute-start.3 = (bf16[32,3712]{1,0:T(8,128)(2,1)S(1)}, bf16[32,3712]{1,0:T(8,128)(2,1)S(1)}, u32[]{:S(2)}, u32[]{:S(2)}) collective-permute-start(bf16[32,3712]{1,0:T(8,128)(2,1)S(1)} %get-tuple-element.74), channel_id=1, source_target_pairs={{0,192},{4,196},{8,200},{12,204},{16,208},{20,212},{24,216},{28,22... | collective-permute-start | bytes 712712 | tf_op jit(solution)/shard_map/ppermute | solution.py:22
  25.9 15.8 %collective-permute-start.4 = (bf16[32,3712]{1,0:T(8,128)(2,1)S(1)}, bf16[32,3712]{1,0:T(8,128)(2,1)S(1)}, u32[]{:S(2)}, u32[]{:S(2)}) collective-permute-start(bf16[32,3712]{1,0:T(8,128)(2,1)S(1)} %get-tuple-element.74), channel_id=1, source_target_pairs={{0,8},{4,12},{8,16},{12,20},{16,24},{20,28},{24,32},{28,36},{32,40... | collective-permute-start | bytes 712712 | tf_op jit(solution)/shard_map/ppermute | solution.py:22
  27.7 15.3 %collective-permute-start.5 = (bf16[32,3712]{1,0:T(8,128)(2,1)S(1)}, bf16[32,3712]{1,0:T(8,128)(2,1)S(1)}, u32[]{:S(2)}, u32[]{:S(2)}) collective-permute-start(bf16[32,3712]{1,0:T(8,128)(2,1)S(1)} %get-tuple-element.74), channel_id=1, source_target_pairs={{0,56},{4,60},{8,0},{12,4},{16,8},{20,12},{24,16},{28,20},{32,24},... | collective-permute-start | bytes 712712 | tf_op jit(solution)/shard_map/ppermute | solution.py:22
  33.6 0.8 copy-start.1
  41.6 5.9 %copy-start.10 = (bf16[160,3712]{1,0:T(8,128)(2,1)S(1)}, bf16[160,3712]{1,0:T(8,128)(2,1)}, u32[]{:S(2)}) copy-start(bf16[160,3712]{1,0:T(8,128)(2,1)} %get-tuple-element.75) | copy-start | bytes 3563524
  41.7 10.4 %collective-permute-start.10 = (bf16[48,3712]{1,0:T(8,128)(2,1)S(1)}, bf16[48,3712]{1,0:T(8,128)(2,1)S(1)}, u32[]{:S(2)}, u32[]{:S(2)}) collective-permute-start(bf16[48,3712]{1,0:T(8,128)(2,1)S(1)} %pad_maximum_fusion.7), channel_id=1, source_target_pairs={{0,64},{4,68},{8,72},{12,76},{16,80},{20,84},{24,88},{28,92},{32,9... | collective-permute-start | bytes 1069064 | tf_op jit(solution)/shard_map/ppermute | solution.py:22
  43.0 9.1 %collective-permute-start.11 = (bf16[48,3712]{1,0:T(8,128)(2,1)S(1)}, bf16[48,3712]{1,0:T(8,128)(2,1)S(1)}, u32[]{:S(2)}, u32[]{:S(2)}) collective-permute-start(bf16[48,3712]{1,0:T(8,128)(2,1)S(1)} %pad_maximum_fusion.8), channel_id=1, source_target_pairs={{0,192},{4,196},{8,200},{12,204},{16,208},{20,212},{24,216},{28,22... | collective-permute-start | bytes 1069064 | tf_op jit(solution)/shard_map/ppermute | solution.py:22
  44.6 12.3 %collective-permute-start.12 = (bf16[64,3712]{1,0:T(8,128)(2,1)S(1)}, bf16[64,3712]{1,0:T(8,128)(2,1)S(1)}, u32[]{:S(2)}, u32[]{:S(2)}) collective-permute-start(bf16[64,3712]{1,0:T(8,128)(2,1)S(1)} %pad_maximum_fusion.1), channel_id=1, source_target_pairs={{0,8},{4,12},{8,16},{12,20},{16,24},{20,28},{24,32},{28,36},{32,40... | collective-permute-start | bytes 1425416 | tf_op jit(solution)/shard_map/ppermute | solution.py:22
  44.8 12.2 %collective-permute-start.13 = (bf16[64,3712]{1,0:T(8,128)(2,1)S(1)}, bf16[64,3712]{1,0:T(8,128)(2,1)S(1)}, u32[]{:S(2)}, u32[]{:S(2)}) collective-permute-start(bf16[64,3712]{1,0:T(8,128)(2,1)S(1)} %pad_maximum_fusion.2), channel_id=1, source_target_pairs={{0,56},{4,60},{8,0},{12,4},{16,8},{20,12},{24,16},{28,20},{32,24},... | collective-permute-start | bytes 1425416 | tf_op jit(solution)/shard_map/ppermute | solution.py:22
  57.0 13.9 %collective-permute-start.14 = (bf16[64,3712]{1,0:T(8,128)(2,1)S(1)}, bf16[64,3712]{1,0:T(8,128)(2,1)S(1)}, u32[]{:S(2)}, u32[]{:S(2)}) collective-permute-start(bf16[64,3712]{1,0:T(8,128)(2,1)S(1)} %pad_maximum_fusion.3), channel_id=1, source_target_pairs={{0,64},{4,68},{8,72},{12,76},{16,80},{20,84},{24,88},{28,92},{32,9... | collective-permute-start | bytes 1425416 | tf_op jit(solution)/shard_map/ppermute | solution.py:22
  57.4 13.8 %collective-permute-start.15 = (bf16[64,3712]{1,0:T(8,128)(2,1)S(1)}, bf16[64,3712]{1,0:T(8,128)(2,1)S(1)}, u32[]{:S(2)}, u32[]{:S(2)}) collective-permute-start(bf16[64,3712]{1,0:T(8,128)(2,1)S(1)} %pad_maximum_fusion.4), channel_id=1, source_target_pairs={{0,192},{4,196},{8,200},{12,204},{16,208},{20,212},{24,216},{28,22... | collective-permute-start | bytes 1425416 | tf_op jit(solution)/shard_map/ppermute | solution.py:22
  60.1 10.8 %collective-permute-start.16 = (bf16[64,3712]{1,0:T(8,128)(2,1)S(1)}, bf16[64,3712]{1,0:T(8,128)(2,1)S(1)}, u32[]{:S(2)}, u32[]{:S(2)}) collective-permute-start(bf16[64,3712]{1,0:T(8,128)(2,1)S(1)} %collective-permute-done.12), channel_id=1, source_target_pairs={{0,8},{4,12},{8,16},{12,20},{16,24},{20,28},{24,32},{28,36},{32,40... | collective-permute-start | bytes 1425416 | tf_op jit(solution)/shard_map/ppermute | solution.py:22
  60.1 9.7 %collective-permute-start.17 = (bf16[64,3712]{1,0:T(8,128)(2,1)S(1)}, bf16[64,3712]{1,0:T(8,128)(2,1)S(1)}, u32[]{:S(2)}, u32[]{:S(2)}) collective-permute-start(bf16[64,3712]{1,0:T(8,128)(2,1)S(1)} %collective-permute-done.13), channel_id=1, source_target_pairs={{0,56},{4,60},{8,0},{12,4},{16,8},{20,12},{24,16},{28,20},{32,24},... | collective-permute-start | bytes 1425416 | tf_op jit(solution)/shard_map/ppermute | solution.py:22
  62.9 8.2 %copy-start.7 = (bf16[224,3712]{1,0:T(8,128)(2,1)}, bf16[224,3712]{1,0:T(8,128)(2,1)S(1)}, u32[]{:S(2)}) copy-start(bf16[224,3712]{1,0:T(8,128)(2,1)S(1)} %constant_dynamic-update-slice_fusion.25) | copy-start | bytes 4988932
  71.0 10.9 %collective-permute-start.18 = (bf16[64,3712]{1,0:T(8,128)(2,1)S(1)}, bf16[64,3712]{1,0:T(8,128)(2,1)S(1)}, u32[]{:S(2)}, u32[]{:S(2)}) collective-permute-start(bf16[64,3712]{1,0:T(8,128)(2,1)S(1)} %pad_maximum_fusion.5), channel_id=1, source_target_pairs={{0,64},{4,68},{8,72},{12,76},{16,80},{20,84},{24,88},{28,92},{32,9... | collective-permute-start | bytes 1425416 | tf_op jit(solution)/shard_map/ppermute | solution.py:22
  71.2 10.8 %collective-permute-start.19 = (bf16[64,3712]{1,0:T(8,128)(2,1)S(1)}, bf16[64,3712]{1,0:T(8,128)(2,1)S(1)}, u32[]{:S(2)}, u32[]{:S(2)}) collective-permute-start(bf16[64,3712]{1,0:T(8,128)(2,1)S(1)} %pad_maximum_fusion.6), channel_id=1, source_target_pairs={{0,192},{4,196},{8,200},{12,204},{16,208},{20,212},{24,216},{28,22... | collective-permute-start | bytes 1425416 | tf_op jit(solution)/shard_map/ppermute | solution.py:22
  74.0 7.8 %collective-permute-start.20 = (bf16[48,3712]{1,0:T(8,128)(2,1)S(1)}, bf16[48,3712]{1,0:T(8,128)(2,1)S(1)}, u32[]{:S(2)}, u32[]{:S(2)}) collective-permute-start(bf16[48,3712]{1,0:T(8,128)(2,1)S(1)} %pad_maximum_fusion.9), channel_id=1, source_target_pairs={{0,8},{4,12},{8,16},{12,20},{16,24},{20,28},{24,32},{28,36},{32,40... | collective-permute-start | bytes 1069064 | tf_op jit(solution)/shard_map/ppermute | solution.py:22
  74.1 7.7 %collective-permute-start.21 = (bf16[48,3712]{1,0:T(8,128)(2,1)S(1)}, bf16[48,3712]{1,0:T(8,128)(2,1)S(1)}, u32[]{:S(2)}, u32[]{:S(2)}) collective-permute-start(bf16[48,3712]{1,0:T(8,128)(2,1)S(1)} %slice.501), channel_id=1, source_target_pairs={{0,56},{4,60},{8,0},{12,4},{16,8},{20,12},{24,16},{28,20},{32,24},... | collective-permute-start | bytes 1069064 | tf_op jit(solution)/shard_map/ppermute | solution.py:22
  77.0 10.6 %copy-start.5 = (bf16[256,3712]{1,0:T(8,128)(2,1)}, bf16[256,3712]{1,0:T(8,128)(2,1)S(1)}, u32[]{:S(2)}) copy-start(bf16[256,3712]{1,0:T(8,128)(2,1)S(1)} %constant_dynamic-update-slice_fusion.43) | copy-start | bytes 5701636
  81.9 6.2 %collective-permute-start.22 = (bf16[32,3712]{1,0:T(8,128)(2,1)S(1)}, bf16[32,3712]{1,0:T(8,128)(2,1)S(1)}, u32[]{:S(2)}, u32[]{:S(2)}) collective-permute-start(bf16[32,3712]{1,0:T(8,128)(2,1)S(1)} %get-tuple-element.81), channel_id=1, source_target_pairs={{0,64},{4,68},{8,72},{12,76},{16,80},{20,84},{24,88},{28,92},{32,9... | collective-permute-start | bytes 712712 | tf_op jit(solution)/shard_map/ppermute | solution.py:22
  82.1 6.1 %collective-permute-start.23 = (bf16[32,3712]{1,0:T(8,128)(2,1)S(1)}, bf16[32,3712]{1,0:T(8,128)(2,1)S(1)}, u32[]{:S(2)}, u32[]{:S(2)}) collective-permute-start(bf16[32,3712]{1,0:T(8,128)(2,1)S(1)} %get-tuple-element.79), channel_id=1, source_target_pairs={{0,192},{4,196},{8,200},{12,204},{16,208},{20,212},{24,216},{28,22... | collective-permute-start | bytes 712712 | tf_op jit(solution)/shard_map/ppermute | solution.py:22
  84.9 6.2 %collective-permute-start.24 = (bf16[32,3712]{1,0:T(8,128)(2,1)S(1)}, bf16[32,3712]{1,0:T(8,128)(2,1)S(1)}, u32[]{:S(2)}, u32[]{:S(2)}) collective-permute-start(bf16[32,3712]{1,0:T(8,128)(2,1)S(1)} %get-tuple-element.80), channel_id=1, source_target_pairs={{0,8},{4,12},{8,16},{12,20},{16,24},{20,28},{24,32},{28,36},{32,40... | collective-permute-start | bytes 712712 | tf_op jit(solution)/shard_map/ppermute | solution.py:22
  84.9 6.3 %collective-permute-start.25 = (bf16[32,3712]{1,0:T(8,128)(2,1)S(1)}, bf16[32,3712]{1,0:T(8,128)(2,1)S(1)}, u32[]{:S(2)}, u32[]{:S(2)}) collective-permute-start(bf16[32,3712]{1,0:T(8,128)(2,1)S(1)} %get-tuple-element.78), channel_id=1, source_target_pairs={{0,56},{4,60},{8,0},{12,4},{16,8},{20,12},{24,16},{28,20},{32,24},... | collective-permute-start | bytes 712712 | tf_op jit(solution)/shard_map/ppermute | solution.py:22
  87.8 11.0 %copy-start.3 = (bf16[224,3712]{1,0:T(8,128)(2,1)}, bf16[224,3712]{1,0:T(8,128)(2,1)S(1)}, u32[]{:S(2)}) copy-start(bf16[224,3712]{1,0:T(8,128)(2,1)S(1)} %constant_dynamic-update-slice_fusion.63) | copy-start | bytes 4988932
  88.2 10.6 %collective-permute-start.26 = (bf16[32,3712]{1,0:T(8,128)(2,1)S(1)}, bf16[32,3712]{1,0:T(8,128)(2,1)S(1)}, u32[]{:S(2)}, u32[]{:S(2)}) collective-permute-start(bf16[32,3712]{1,0:T(8,128)(2,1)S(1)} %concatenate.179), channel_id=1, source_target_pairs={{0,72},{4,76},{8,80},{12,84},{16,88},{20,92},{24,96},{28,100},{32,... | collective-permute-start | bytes 712712 | tf_op jit(solution)/shard_map/ppermute | solution.py:22
  98.8 1.0 copy-start.11
  106.8 5.9 %copy-start = (bf16[8,128,3584]{2,1,0:T(8,128)(2,1)S(1)}, bf16[8,128,3584]{2,1,0:T(8,128)(2,1)}, u32[]{:S(2)}) copy-start(bf16[8,128,3584]{2,1,0:T(8,128)(2,1)} %pad_maximum_fusion) | copy-start | bytes 22020100
  106.8 5.9 %copy-start.8 = (bf16[224,3712]{1,0:T(8,128)(2,1)S(1)}, bf16[224,3712]{1,0:T(8,128)(2,1)}, u32[]{:S(2)}) copy-start(bf16[224,3712]{1,0:T(8,128)(2,1)} %copy-done.7) | copy-start | bytes 4988932
  112.7 2.5 %copy-start.6 = (bf16[256,3712]{1,0:T(8,128)(2,1)S(1)}, bf16[256,3712]{1,0:T(8,128)(2,1)}, u32[]{:S(2)}) copy-start(bf16[256,3712]{1,0:T(8,128)(2,1)} %copy-done.5) | copy-start | bytes 5701636
  115.2 2.1 %copy-start.4 = (bf16[224,3712]{1,0:T(8,128)(2,1)S(1)}, bf16[224,3712]{1,0:T(8,128)(2,1)}, u32[]{:S(2)}) copy-start(bf16[224,3712]{1,0:T(8,128)(2,1)} %copy-done.3) | copy-start | bytes 4988932
  117.3 2.5 %copy-start.12 = (bf16[160,3712]{1,0:T(8,128)(2,1)S(1)}, bf16[160,3712]{1,0:T(8,128)(2,1)}, u32[]{:S(2)}) copy-start(bf16[160,3712]{1,0:T(8,128)(2,1)} %copy-done.11) | copy-start | bytes 3563524

commit v3 on v2

--- a/solution.py
+++ b/solution.py
@@ -1,7 +1,11 @@
+import functools
+
 import jax
 import jax.numpy as jnp
 import numpy as np
 from jax import lax
+from jax.experimental import pallas as pl
+from jax.experimental.pallas import tpu as pltpu
 from jax.sharding import PartitionSpec as P
 
 EXACT = lax.Precision.HIGHEST
@@ -62,6 +66,99 @@
 ]
 
 
+def scores_kernel(places, sizes, where, q_own, q_other, *refs):
+    slices, pieces = refs[:NX], refs[NX : NX + len(sizes)]
+    out, seq, q_buf, a_buf, g_buf, w_buf, q_sem, a_sem, g_sem = refs[NX + len(sizes) :]
+    queries, rows, half = q_other.shape
+    tokens = sum(sizes) // len(places)
+    start = pl.multiple_of(where[2] * half, 128)
+    q_copies = [
+        [
+            pltpu.make_async_copy(
+                q_own.at[q, :, pl.ds(start, half)], q_buf.at[0, q], q_sem.at[0, q]
+            )
+            for q in range(queries)
+        ],
+        [
+            pltpu.make_async_copy(q_other.at[q], q_buf.at[1, q], q_sem.at[1, q])
+            for q in range(queries)
+        ],
+    ]
+    g_copies = [
+        pltpu.make_async_copy(g, g_buf.at[k], g_sem.at[k]) for k, g in enumerate(slices)
+    ]
+    count, a_copies = 0, []
+    for i, (piece, size) in enumerate(zip(pieces, sizes)):
+        a_copies.append(
+            pltpu.make_async_copy(piece, a_buf.at[pl.ds(count, size)], a_sem.at[i])
+        )
+        count += size
+    for copy in g_copies + a_copies + q_copies[0] + q_copies[1]:
+        copy.start()
+    for copy in g_copies:
+        copy.wait()
+    for i, ((ox, oz), h) in enumerate(places):
+        u = lax.rem(where[0] + (NX - ox), NX)
+        v = lax.rem(where[1] + (NZ - oz), NZ)
+        at = pl.multiple_of(v * (2 * tokens) + h * tokens, tokens)
+        w_buf[pl.ds(i * tokens, tokens)] = g_buf[u, pl.ds(at, tokens)]
+    weights = w_buf[...].astype(jnp.float32).T
+    for copy in a_copies:
+        copy.wait()
+    total = [jnp.zeros((1, count), jnp.float32) for _ in range(queries)]
+    for p in range(2):
+        for copy in q_copies[p]:
+            copy.wait()
+        inner = lax.dot_general(
+            q_buf[p].reshape(queries * rows, half),
+            a_buf[:, :half],
+            (((1,), (1,)), ((), ())),
+            preferred_element_type=jnp.float32,
+        )
+        for q in range(queries):
+            weighed = inner[q * rows : (q + 1) * rows] * weights[p * rows : (p + 1) * rows]
+            total[q] = total[q] + jnp.sum(weighed, axis=0, keepdims=True)
+    scores = jnp.concatenate(total + [jnp.zeros((8 - queries, count), jnp.float32)], 0)
+    out[...] = scores
+    ids = a_buf[:, half:].astype(jnp.float32)
+    lane = lax.broadcasted_iota(jnp.int32, (count, 128), 1).astype(jnp.float32)
+    onehot = jnp.where(ids == lane, 1.0, 0.0)
+    seq[...] = jnp.dot(scores, onehot, precision=EXACT, preferred_element_type=jnp.float32)
+
+
+def piece_scores(where, q_own, q_other, slices, pieces, places):
+    sizes = [piece.shape[0] for piece in pieces]
+    count = sum(sizes)
+    queries, rows, half = q_other.shape
+    anywhere = pl.BlockSpec(memory_space=pl.ANY)
+    whole = pl.BlockSpec(memory_space=pltpu.VMEM)
+    return pl.pallas_call(
+        functools.partial(scores_kernel, places, sizes),
+        out_shape=(
+            jax.ShapeDtypeStruct((8, count), jnp.float32),
+            jax.ShapeDtypeStruct((8, 128), jnp.float32),
+        ),
+        in_specs=[pl.BlockSpec(memory_space=pltpu.SMEM)] + [anywhere] * (2 + NX + len(pieces)),
+        out_specs=[whole, whole],
+        scratch_shapes=[
+            pltpu.VMEM((2, queries, rows, half), jnp.bfloat16),
+            pltpu.VMEM((count, half + 128), jnp.bfloat16),
+            pltpu.VMEM((NX,) + slices[0].shape, jnp.bfloat16),
+            pltpu.VMEM((count, 2 * rows), jnp.bfloat16),
+            pltpu.SemaphoreType.DMA((2, queries)),
+            pltpu.SemaphoreType.DMA((len(pieces),)),
+            pltpu.SemaphoreType.DMA((NX,)),
+        ],
+        compiler_params=pltpu.CompilerParams(vmem_limit_bytes=24 << 20),
+        cost_estimate=pl.CostEstimate(
+            flops=4 * queries * rows * half * count,
+            bytes_accessed=4 * queries * rows * half + 2 * half * count,
+            transcendentals=0,
+        ),
+        name="scores",
+    )(where, q_own, q_other, *slices, *pieces)
+
+
 def body(query_grads, out_grads, activations, seq_ids):
     queries, rows_here, width = query_grads.shape
     half = width // 2
@@ -80,47 +177,45 @@
     other = swap(cat([columns(activations, 1 - core), ids], 1))
     own = jnp.where(core == 0, cat([mine, other]), cat([other, mine]))
 
-    grads = cat([columns(query_grads, core), swap(columns(query_grads, 1 - core))])
-    grads = grads.reshape(2 * queries * rows_here, half)
-    slices = cat([out_grads, swap(out_grads)], 1)
-    slices = jnp.stack([slices] + [from_col(slices, k, cols) for k in range(1, cols)])
-    slices = lax.dynamic_slice_in_dim(cat([slices, slices]), (x - y) % NX, NX)
-    slices = slices.reshape(NX, NZ, 2, tokens, 2 * rows_here)
-    slices = lax.dynamic_slice_in_dim(cat([slices, slices], 1), z, NZ, 1)
+    own, query_grads = lax.optimization_barrier((own, query_grads))
+
+    q_other = columns(query_grads, 1 - core)
+    slices = [cat([out_grads, swap(out_grads)], 1)]
+    where = jnp.stack([(x - y) % NX, z, core]).astype(jnp.int32)
 
     held = {((0, 0), h): own[h * tokens : (h + 1) * tokens] for h in F}
-    slots, scores, came_ids = [], [], []
-
-    def work(arrays, places):
-        block = cat(arrays)
-        weights = cat([slices[-ox % NX, -oz % NZ, h] for (ox, oz), h in places])
-        inner = lax.dot_general(
-            grads, block[:, :half], (((1,), (1,)), ((), ())), preferred_element_type=jnp.float32
-        )
-        inner = inner.reshape(2, queries, rows_here, block.shape[0])
-        weights = weights.astype(jnp.float32).T.reshape(2, 1, rows_here, block.shape[0])
-        scores.append(jnp.sum(inner * weights, axis=(0, 2)))
-        came_ids.append(block[:, half])
-        slots.extend(places)
-
+    slots, scores, by_seq = [], [], []
     arrays, places = [own], [((0, 0), h) for h in F]
-    for moves in ROUNDS:
-        came = []
-        for (dx, dz), load in moves:
-            sent = cat([cat([held[src, h] for h in part]) for src, part, _ in load])
-            came.append((shift(sent, dx, dz), [(dst, h) for _, part, dst in load for h in part]))
-        for array, names in came:
+    for number, moves in enumerate(ROUNDS):
+        sent = [cat([cat([held[src, h] for h in part]) for src, part, _ in load]) for _, load in moves]
+        if number == 1:
+            sent, slices, q_other = lax.optimization_barrier((sent, slices, q_other))
+            q_other = swap(q_other)
+            slices += [from_col(slices[0], k, cols) for k in range(1, cols)]
+        if number == 2:
+            sent, slices, q_other = lax.optimization_barrier((sent, slices, q_other))
+        if number > 2:
+            sent, scores[-1] = lax.optimization_barrier((sent, scores[-1]))
+        if number > 1:
+            part, seq = piece_scores(where, query_grads, q_other, slices, arrays, places)
+            scores.append(part)
+            by_seq.append(seq)
+            slots += places
+            arrays, places = [], []
+        for ((dx, dz), load), block in zip(moves, sent):
+            came = shift(block, dx, dz)
+            names = [(dst, h) for _, part, dst in load for h in part]
             for i, name in enumerate(names):
-                held[name] = array[i * tokens : (i + 1) * tokens]
-            arrays.append(array)
+                held[name] = came[i * tokens : (i + 1) * tokens]
+            arrays.append(came)
             places += names
-        work(arrays, places)
-        arrays, places = [], []
-
-    partial = cat(scores, 1)
-    all_ids = cat(came_ids).astype(jnp.int32)
-    onehot = all_ids[:, None] == jnp.arange(seq_count, dtype=jnp.int32)[None, :]
-    partial_seq = jnp.dot(partial, onehot.astype(jnp.float32), precision=EXACT)
+    part, seq = piece_scores(where, query_grads, q_other, slices, arrays, places)
+    scores.append(part)
+    by_seq.append(seq)
+    slots += places
+
+    partial = cat(scores, 1)[:queries]
+    partial_seq = sum(by_seq[1:], by_seq[0])[:queries, :seq_count]
     far = np.array([(NX - ox, NZ - oz, h) for (ox, oz), h in slots], np.int32).T
     owner = ((x + far[0]) % NX * NZ + (z + far[1]) % NZ) * 2 + far[2]
     place = owner[:, None] == jnp.arange(rows, dtype=jnp.int32)[None, :]

time: 156 us -> 136 us (0.87)
  Pallas kernels: 0 us -> 34.1 us
  waiting for transfers between devices: 38.8 us -> 17.3 us
  matrix products: 16.3 us -> 0.29 us
  local copies, waits for them, and re-layouts: 19.7 us -> 13.7 us
  other arithmetic: 8.54 us -> 4.09 us
  blocking collectives: 29.7 us -> 26.6 us
  starting transfers between devices: 40.9 us -> 38.6 us
    pallas_call x0 -> x4, Pallas kernels: none -> 34.1 us  [piece_scores(): pl.pallas_call(functools.partial(scores_kernel, places, sizes), out_shape...]
    ppermute x21, waiting for transfers between devices: 32.3 us -> 12.6 us  [shift(): return lax.ppermute(block, 'row', pairs)]
    dot_general x6 -> x0, matrix products: 16 us -> none  [the longest x5 15.6 us: work(): lax.dot_general(grads, block[:, :half], (((1,), (1,)), ((), ())), preferr...]
    ppermute x21, starting transfers between devices: 35 us -> 27.6 us  [shift(): return lax.ppermute(block, 'row', pairs)]
    ppermute x3, waiting for transfers between devices: 5.39 us -> 0.43 us  [swap(): return lax.ppermute(block, 'row', [(i, i ^ 1) for i in range(NX * NZ * 2)])]
    concatenate x15, other arithmetic: 7.41 us -> 3 us  [cat(): return parts[0] if len(parts) == 1 else jnp.concatenate(parts, axis)]
    ppermute x3, starting transfers between devices: 2.12 us -> 6.12 us  [from_col(): lax.ppermute(block, 'col', [(i, (i - ahead) % cols) for i in range(cols)])]
    dynamic_slice x2, local copies, waits for them, and re-layouts: 6.74 us -> 3.24 us  [columns(): return lax.dynamic_slice(array, start, array.shape[:-1] + (half,))]
  transfers between devices with their start and end apart: 27 -> 27, of which waited for: 11 -> 8; matrix products, arithmetic and copies ran while one was open for 7% -> 5% of each run, Pallas kernels for 0% -> 19%
where the time goes in v3:
time: 136 us
  starting transfers between devices  38.6 us (28%)
  Pallas kernels  34.1 us (25%)
  blocking collectives  26.6 us (20%)
  waiting for transfers between devices  17.3 us (13%)
  local copies, waits for them, and re-layouts  13.7 us (10%)
  other arithmetic  4.09 us (3%)
    pallas_call x4, Pallas kernels, piece_scores(): pl.pallas_call(functools.partial(scores_kernel, places, sizes), out_shape...  34.1 us
    ppermute x21, starting transfers between devices, shift(): return lax.ppermute(block, 'row', pairs)  27.6 us
    all_to_all x1, blocking collectives, body(): arrived = lax.all_to_all(parts, ('row', 'col'), 0, 0, tiled=True)  26.6 us
    ppermute x21, waiting for transfers between devices, shift(): return lax.ppermute(block, 'row', pairs)  12.6 us
    unnamed x16, local copies, waits for them, and re-layouts  7.93 us
    ppermute x3, starting transfers between devices, from_col(): lax.ppermute(block, 'col', [(i, (i - ahead) % cols) for i in range(cols)])  6.12 us
    ppermute x3, starting transfers between devices, swap(): return lax.ppermute(block, 'row', [(i, i ^ 1) for i in range(NX * NZ * 2)])  4.82 us
    ppermute x3, waiting for transfers between devices, from_col(): lax.ppermute(block, 'col', [(i, (i - ahead) % cols) for i in range(cols)])  4.3 us
  transfers between devices with their start and end apart: 27, of which 8 were waited for; matrix products, arithmetic and copies ran while one was open for 5% of the time, Pallas kernels for 19%

profile of v3, /device:TPU:1, one launch (start us, length us, event | category | flops | bytes accessed | tf_op | source)
XLA Modules:
  0.0 135.8 jit_solution(563548756392012753)
XLA Ops:
  0.6 3.3 %collective-permute-start.5 = (bf16[256,128]{1,0:T(8,128)(2,1)}, bf16[256,128]{1,0:T(8,128)(2,1)S(1)}, u32[]{:S(2)}, u32[]{:S(2)}) collective-permute-start(bf16[256,128]{1,0:T(8,128)(2,1)} %param.8), channel_id=1, source_target_pairs={{0,4},{4,0},{8,12},{12,8},{16,20},{20,16},{24,28},{28,24},{32,36},... | collective-permute-start | bytes 196616 | tf_op jit(solution)/shard_map/ppermute | solution.py:30
  4.0 0.7 convert_element_type.5
  4.6 1.0 constant_dynamic-slice_fusion.2
  5.7 0.1 collective-permute-start
  5.8 0.9 pad_maximum_fusion.13.refs_0_
  6.7 0.4 collective-permute-done
  7.2 2.4 %collective-permute-start.3 = (bf16[32,3712]{1,0:T(8,128)(2,1)S(1)}, bf16[32,3712]{1,0:T(8,128)(2,1)S(1)}, u32[]{:S(2)}, u32[]{:S(2)}) collective-permute-start(bf16[32,3712]{1,0:T(8,128)(2,1)S(1)} %maximum_select_fusion.refs_4_), channel_id=1, source_target_pairs={{0,192},{4,196},{8,200},{12,204},{16,208},{20,212},{24,216},{28,22... | collective-permute-start | bytes 712712 | tf_op jit(solution)/shard_map/ppermute | solution.py:26
  9.6 4.0 %collective-permute-start.4 = (bf16[32,3712]{1,0:T(8,128)(2,1)S(1)}, bf16[32,3712]{1,0:T(8,128)(2,1)S(1)}, u32[]{:S(2)}, u32[]{:S(2)}) collective-permute-start(bf16[32,3712]{1,0:T(8,128)(2,1)S(1)} %maximum_select_fusion.refs_4_), channel_id=1, source_target_pairs={{0,56},{4,60},{8,0},{12,4},{16,8},{20,12},{24,16},{28,20},{32,24},... | collective-permute-start | bytes 712712 | tf_op jit(solution)/shard_map/ppermute | solution.py:26
  13.6 2.3 %constant_dynamic-slice_fusion = bf16[4,128,3584]{2,1,0:T(8,128)(2,1)S(1)} fusion(bf16[4,128,7168]{2,1,0:T(8,128)(2,1)} %q_own.3, s32[]{:T(128)S(6)} %select_n.55), kind=kLoop, calls=%fused_computation.31 | loop fusion | bytes 7340036 | tf_op jit(solution)/shard_map/dynamic_slice | solution.py:173
  15.9 1.5 %collective-permute-done.1.refs_5_ = bf16[32,3712]{1,0:T(8,128)(2,1)S(1)} collective-permute-done((bf16[32,3712]{1,0:T(8,128)(2,1)S(1)}, bf16[32,3712]{1,0:T(8,128)(2,1)S(1)}, u32[]{:S(2)}, u32[]{:S(2)}) %collective-permute-start.1) | collective-permute-done | bytes 237600 | tf_op jit(solution)/shard_map/ppermute | solution.py:26
  17.5 0.9 collective-permute-done.4.refs_8_
  18.5 1.4 %collective-permute-start.13 = (bf16[4,128,3584]{2,1,0:T(8,128)(2,1)S(1)}, bf16[4,128,3584]{2,1,0:T(8,128)(2,1)S(1)}, u32[]{:S(2)}, u32[]{:S(2)}) collective-permute-start(bf16[4,128,3584]{2,1,0:T(8,128)(2,1)S(1)} %constant_dynamic-slice_fusion), channel_id=1, source_target_pairs={{0,4},{4,0},{8,12},{12,8},{16,20},{20,16},{24,28},{28,24},{32,36},... | collective-permute-start | bytes 11010056 | tf_op jit(solution)/shard_map/ppermute | solution.py:30
  19.8 1.1 collective-permute-start.8
  20.9 2.4 %collective-permute-start.7 = (bf16[64,3712]{1,0:T(8,128)(2,1)S(1)}, bf16[64,3712]{1,0:T(8,128)(2,1)S(1)}, u32[]{:S(2)}, u32[]{:S(2)}) collective-permute-start(bf16[64,3712]{1,0:T(8,128)(2,1)S(1)} %pad_maximum_fusion.1), channel_id=1, source_target_pairs={{0,56},{4,60},{8,0},{12,4},{16,8},{20,12},{24,16},{28,20},{32,24},... | collective-permute-start | bytes 1425416 | tf_op jit(solution)/shard_map/ppermute | solution.py:26
  23.3 2.6 %collective-permute-start.9 = (bf16[48,3712]{1,0:T(8,128)(2,1)S(1)}, bf16[48,3712]{1,0:T(8,128)(2,1)S(1)}, u32[]{:S(2)}, u32[]{:S(2)}) collective-permute-start(bf16[48,3712]{1,0:T(8,128)(2,1)S(1)} %pad_maximum_fusion.7), channel_id=1, source_target_pairs={{0,192},{4,196},{8,200},{12,204},{16,208},{20,212},{24,216},{28,22... | collective-permute-start | bytes 1069064 | tf_op jit(solution)/shard_map/ppermute | solution.py:26
  25.9 7.2 %collective-permute-done.9.refs_10_ = bf16[48,3712]{1,0:T(8,128)(2,1)S(1)} collective-permute-done((bf16[48,3712]{1,0:T(8,128)(2,1)S(1)}, bf16[48,3712]{1,0:T(8,128)(2,1)S(1)}, u32[]{:S(2)}, u32[]{:S(2)}) %collective-permute-start.9) | collective-permute-done | bytes 356384 | tf_op jit(solution)/shard_map/ppermute | solution.py:26
  33.2 2.7 %collective-permute-start.10 = (bf16[256,256]{1,0:T(8,128)(2,1)S(1)}, bf16[256,256]{1,0:T(8,128)(2,1)S(1)}, u32[]{:S(2)}, u32[]{:S(2)}) collective-permute-start(bf16[256,256]{1,0:T(8,128)(2,1)S(1)} %pad_maximum_fusion.13.refs_0_), channel_id=1, source_target_pairs={{0,3},{1,0},{2,1},{3,2},{4,7},{5,4},{6,5},{7,6},{8,11},{9,8},{10,9... | collective-permute-start | bytes 393224 | tf_op jit(solution)/shard_map/ppermute | solution.py:34
  35.9 0.3 collective-permute-done.6.refs_9_
  36.2 2.9 %collective-permute-start.11 = (bf16[256,256]{1,0:T(8,128)(2,1)S(1)}, bf16[256,256]{1,0:T(8,128)(2,1)S(1)}, u32[]{:S(2)}, u32[]{:S(2)}) collective-permute-start(bf16[256,256]{1,0:T(8,128)(2,1)S(1)} %pad_maximum_fusion.13.refs_0_), channel_id=1, source_target_pairs={{0,2},{1,3},{2,0},{3,1},{4,6},{5,7},{6,4},{7,5},{8,10},{9,11},{10,... | collective-permute-start | bytes 393224 | tf_op jit(solution)/shard_map/ppermute | solution.py:34
  39.2 0.5 collective-permute-start.12
  39.7 0.8 pad_maximum_fusion.3
  40.6 0.8 pad_maximum_fusion.2
  41.4 0.1 collective-permute-done.11.refs_2_
  41.6 4.2 %collective-permute-done.12.refs_3_ = bf16[256,256]{1,0:T(8,128)(2,1)S(1)} collective-permute-done((bf16[256,256]{1,0:T(8,128)(2,1)S(1)}, bf16[256,256]{1,0:T(8,128)(2,1)S(1)}, u32[]{:S(2)}, u32[]{:S(2)}) %collective-permute-start.12) | collective-permute-done | bytes 131104 | tf_op jit(solution)/shard_map/ppermute | solution.py:34
  45.7 1.8 %copy-done.1 = bf16[4,128,3584]{2,1,0:T(8,128)(2,1)} copy-done((bf16[4,128,3584]{2,1,0:T(8,128)(2,1)}, bf16[4,128,3584]{2,1,0:T(8,128)(2,1)S(1)}, u32[]{:S(2)}) %copy-start.1) | copy-done | bytes 3670040
  47.6 2.9 %collective-permute-start.15 = (bf16[64,3712]{1,0:T(8,128)(2,1)S(1)}, bf16[64,3712]{1,0:T(8,128)(2,1)S(1)}, u32[]{:S(2)}, u32[]{:S(2)}) collective-permute-start(bf16[64,3712]{1,0:T(8,128)(2,1)S(1)} %collective-permute-done.7.refs_12_), channel_id=1, source_target_pairs={{0,56},{4,60},{8,0},{12,4},{16,8},{20,12},{24,16},{28,20},{32,24},... | collective-permute-start | bytes 1425416 | tf_op jit(solution)/shard_map/ppermute | solution.py:26
  50.5 2.6 %collective-permute-start.17 = (bf16[64,3712]{1,0:T(8,128)(2,1)}, bf16[64,3712]{1,0:T(8,128)(2,1)S(1)}, u32[]{:S(2)}, u32[]{:S(2)}) collective-permute-start(bf16[64,3712]{1,0:T(8,128)(2,1)} %pad_maximum_fusion.3), channel_id=1, source_target_pairs={{0,192},{4,196},{8,200},{12,204},{16,208},{20,212},{24,216},{28,22... | collective-permute-start | bytes 1425416 | tf_op jit(solution)/shard_map/ppermute | solution.py:26
  53.1 3.1 %copy-done = bf16[4,128,7168]{2,1,0:T(8,128)(2,1)S(1)} copy-done((bf16[4,128,7168]{2,1,0:T(8,128)(2,1)S(1)}, bf16[4,128,7168]{2,1,0:T(8,128)(2,1)}, u32[]{:S(2)}) %copy-start) | copy-done | bytes 7340056
  56.1 2.0 %copy-done.2 = bf16[4,128,3584]{2,1,0:T(8,128)(2,1)S(1)} copy-done((bf16[4,128,3584]{2,1,0:T(8,128)(2,1)S(1)}, bf16[4,128,3584]{2,1,0:T(8,128)(2,1)}, u32[]{:S(2)}) %copy-start.2) | copy-done | bytes 3670040
  58.2 1.0 copy-done.4
  59.2 9.6 %scores.4 = (f32[8,384]{1,0:T(8,128)S(1)}, f32[8,128]{1,0:T(8,128)S(1)}) custom-call(s32[3]{0:T(128)S(1)} %pad_add_fusion.where, bf16[4,128,7168]{2,1,0:T(8,128)(2,1)S(1)} %copy-done, bf16[4,128,3584]{2,1,0:T(8,128)(2,1)S(1)} %copy-done.2, bf16[256,256]{1,0:T(8,128)(2,1)S(1)} %pad_maximum_fusion.13.refs_0_, ...), custom_call_target="tpu_custom_call" | custom-call | flops 2818572288 | bytes 10092544 | tf_op jit(solution)/shard_map/scores/pallas_call | solution.py:135
  69.1 0.2 collective-permute-start.19
  69.3 2.8 %collective-permute-start.21 = (bf16[64,3712]{1,0:T(8,128)(2,1)S(1)}, bf16[64,3712]{1,0:T(8,128)(2,1)S(1)}, u32[]{:S(2)}, u32[]{:S(2)}) collective-permute-start(bf16[64,3712]{1,0:T(8,128)(2,1)S(1)} %pad_maximum_fusion.5), channel_id=1, source_target_pairs={{0,192},{4,196},{8,200},{12,204},{16,208},{20,212},{24,216},{28,22... | collective-permute-start | bytes 1425416 | tf_op jit(solution)/shard_map/ppermute | solution.py:26
  72.1 1.3 collective-permute-start.20
  73.4 8.2 %scores.5 = (f32[8,256]{1,0:T(8,128)S(1)}, f32[8,128]{1,0:T(8,128)S(1)}) custom-call(s32[3]{0:T(128)S(1)} %pad_add_fusion.where, bf16[4,128,7168]{2,1,0:T(8,128)(2,1)S(1)} %copy-done, bf16[4,128,3584]{2,1,0:T(8,128)(2,1)S(1)} %copy-done.2, bf16[256,256]{1,0:T(8,128)(2,1)S(1)} %pad_maximum_fusion.13.refs_0_, ...), custom_call_target="tpu_custom_call" | custom-call | flops 1879048192 | bytes 9175040 | tf_op jit(solution)/shard_map/scores/pallas_call | solution.py:135
  81.9 2.7 %collective-permute-start.23 = (bf16[32,3712]{1,0:T(8,128)(2,1)S(1)}, bf16[32,3712]{1,0:T(8,128)(2,1)S(1)}, u32[]{:S(2)}, u32[]{:S(2)}) collective-permute-start(bf16[32,3712]{1,0:T(8,128)(2,1)S(1)} %get-tuple-element.65), channel_id=1, source_target_pairs={{0,192},{4,196},{8,200},{12,204},{16,208},{20,212},{24,216},{28,22... | collective-permute-start | bytes 712712 | tf_op jit(solution)/shard_map/ppermute | solution.py:26
  84.5 0.1 collective-permute-start.24
  84.6 2.6 %collective-permute-start.25 = (bf16[32,3712]{1,0:T(8,128)(2,1)S(1)}, bf16[32,3712]{1,0:T(8,128)(2,1)S(1)}, u32[]{:S(2)}, u32[]{:S(2)}) collective-permute-start(bf16[32,3712]{1,0:T(8,128)(2,1)S(1)} %get-tuple-element.67), channel_id=1, source_target_pairs={{0,56},{4,60},{8,0},{12,4},{16,8},{20,12},{24,16},{28,20},{32,24},... | collective-permute-start | bytes 712712 | tf_op jit(solution)/shard_map/ppermute | solution.py:26
  87.3 7.9 %scores.6 = (f32[8,224]{1,0:T(8,128)S(1)}, f32[8,128]{1,0:T(8,128)S(1)}) custom-call(s32[3]{0:T(128)S(1)} %pad_add_fusion.where, bf16[4,128,7168]{2,1,0:T(8,128)(2,1)S(1)} %copy-done, bf16[4,128,3584]{2,1,0:T(8,128)(2,1)S(1)} %copy-done.2, bf16[256,256]{1,0:T(8,128)(2,1)S(1)} %pad_maximum_fusion.13.refs_0_, ...), custom_call_target="tpu_custom_call" | custom-call | flops 1644167168 | bytes 8945664 | tf_op jit(solution)/shard_map/scores/pallas_call | solution.py:135
  95.2 2.6 %collective-permute-done.26.refs_8_ = bf16[32,3712]{1,0:T(8,128)(2,1)S(1)} collective-permute-done((bf16[32,3712]{1,0:T(8,128)(2,1)S(1)}, bf16[32,3712]{1,0:T(8,128)(2,1)S(1)}, u32[]{:S(2)}, u32[]{:S(2)}) %collective-permute-start.26) | collective-permute-done | bytes 237600 | tf_op jit(solution)/shard_map/ppermute | solution.py:26
  97.8 8.5 %scores.7 = (f32[8,160]{1,0:T(8,128)S(1)}, f32[8,128]{1,0:T(8,128)S(1)}) custom-call(s32[3]{0:T(128)S(1)} %pad_add_fusion.where, bf16[4,128,7168]{2,1,0:T(8,128)(2,1)S(1)} %copy-done, bf16[4,128,3584]{2,1,0:T(8,128)(2,1)S(1)} %copy-done.2, bf16[256,256]{1,0:T(8,128)(2,1)S(1)} %pad_maximum_fusion.13.refs_0_, ...), custom_call_target="tpu_custom_call" | custom-call | flops 1174405120 | bytes 8486912 | tf_op jit(solution)/shard_map/scores/pallas_call | solution.py:135
  106.5 0.1 reshape.41
  106.8 0.3 fusion.1
  107.1 0.4 all_to_all.8
  107.5 26.6 %all_to_all.10 = f32[256,1,192]{2,1,0:T(1,128)S(1)} all-to-all(f32[256,1,192]{2,1,0:T(1,128)S(1)} %all_to_all.8), channel_id=1, replica_groups=mesh['row'=64,'col'=4] {'row','col'}, dimensions={0} | all-to-all | bytes 393216 | tf_op jit(solution)/shard_map/all_to_all | solution.py:233
  134.1 0.3 reduce_sum.9
  134.5 0.7 reshape.42
  135.1 0.7 reshape.43
  (83 shorter events, 1.6 us)
Async XLA Ops:
  0.6 5.2 %collective-permute-start.5 = (bf16[256,128]{1,0:T(8,128)(2,1)}, bf16[256,128]{1,0:T(8,128)(2,1)S(1)}, u32[]{:S(2)}, u32[]{:S(2)}) collective-permute-start(bf16[256,128]{1,0:T(8,128)(2,1)} %param.8), channel_id=1, source_target_pairs={{0,4},{4,0},{8,12},{12,8},{16,20},{20,16},{24,28},{28,24},{32,36},... | collective-permute-start | bytes 196616 | tf_op jit(solution)/shard_map/ppermute | solution.py:30
  5.7 1.4 %collective-permute-start = (bf16[16,3712]{1,0:T(8,128)(2,1)S(1)}, bf16[16,3712]{1,0:T(8,128)(2,1)S(1)}, u32[]{:S(2)}, u32[]{:S(2)}) collective-permute-start(bf16[16,3712]{1,0:T(8,128)(2,1)S(1)} %pad_maximum_fusion.14), channel_id=1, source_target_pairs={{0,4},{4,0},{8,12},{12,8},{16,20},{20,16},{24,28},{28,24},{32,36},... | collective-permute-start | bytes 356360 | tf_op jit(solution)/shard_map/ppermute | solution.py:30
  7.1 10.3 %collective-permute-start.2 = (bf16[32,3712]{1,0:T(8,128)(2,1)S(1)}, bf16[32,3712]{1,0:T(8,128)(2,1)S(1)}, u32[]{:S(2)}, u32[]{:S(2)}) collective-permute-start(bf16[32,3712]{1,0:T(8,128)(2,1)S(1)} %maximum_select_fusion.refs_4_), channel_id=1, source_target_pairs={{0,8},{4,12},{8,16},{12,20},{16,24},{20,28},{24,32},{28,36},{32,40... | collective-permute-start | bytes 712712 | tf_op jit(solution)/shard_map/ppermute | solution.py:26
  7.2 8.7 %collective-permute-start.3 = (bf16[32,3712]{1,0:T(8,128)(2,1)S(1)}, bf16[32,3712]{1,0:T(8,128)(2,1)S(1)}, u32[]{:S(2)}, u32[]{:S(2)}) collective-permute-start(bf16[32,3712]{1,0:T(8,128)(2,1)S(1)} %maximum_select_fusion.refs_4_), channel_id=1, source_target_pairs={{0,192},{4,196},{8,200},{12,204},{16,208},{20,212},{24,216},{28,22... | collective-permute-start | bytes 712712 | tf_op jit(solution)/shard_map/ppermute | solution.py:26
  9.6 7.8 %collective-permute-start.1 = (bf16[32,3712]{1,0:T(8,128)(2,1)S(1)}, bf16[32,3712]{1,0:T(8,128)(2,1)S(1)}, u32[]{:S(2)}, u32[]{:S(2)}) collective-permute-start(bf16[32,3712]{1,0:T(8,128)(2,1)S(1)} %maximum_select_fusion.refs_4_), channel_id=1, source_target_pairs={{0,64},{4,68},{8,72},{12,76},{16,80},{20,84},{24,88},{28,92},{32,9... | collective-permute-start | bytes 712712 | tf_op jit(solution)/shard_map/ppermute | solution.py:26
  9.6 8.7 %collective-permute-start.4 = (bf16[32,3712]{1,0:T(8,128)(2,1)S(1)}, bf16[32,3712]{1,0:T(8,128)(2,1)S(1)}, u32[]{:S(2)}, u32[]{:S(2)}) collective-permute-start(bf16[32,3712]{1,0:T(8,128)(2,1)S(1)} %maximum_select_fusion.refs_4_), channel_id=1, source_target_pairs={{0,56},{4,60},{8,0},{12,4},{16,8},{20,12},{24,16},{28,20},{32,24},... | collective-permute-start | bytes 712712 | tf_op jit(solution)/shard_map/ppermute | solution.py:26
  18.5 27.3 %collective-permute-start.13 = (bf16[4,128,3584]{2,1,0:T(8,128)(2,1)S(1)}, bf16[4,128,3584]{2,1,0:T(8,128)(2,1)S(1)}, u32[]{:S(2)}, u32[]{:S(2)}) collective-permute-start(bf16[4,128,3584]{2,1,0:T(8,128)(2,1)S(1)} %constant_dynamic-slice_fusion), channel_id=1, source_target_pairs={{0,4},{4,0},{8,12},{12,8},{16,20},{20,16},{24,28},{28,24},{32,36},... | collective-permute-start | bytes 11010056 | tf_op jit(solution)/shard_map/ppermute | solution.py:30
  19.8 19.3 %collective-permute-start.8 = (bf16[64,3712]{1,0:T(8,128)(2,1)S(1)}, bf16[64,3712]{1,0:T(8,128)(2,1)S(1)}, u32[]{:S(2)}, u32[]{:S(2)}) collective-permute-start(bf16[64,3712]{1,0:T(8,128)(2,1)S(1)} %pad_maximum_fusion), channel_id=1, source_target_pairs={{0,8},{4,12},{8,16},{12,20},{16,24},{20,28},{24,32},{28,36},{32,40... | collective-permute-start | bytes 1425416 | tf_op jit(solution)/shard_map/ppermute | solution.py:26
  20.9 18.8 %collective-permute-start.7 = (bf16[64,3712]{1,0:T(8,128)(2,1)S(1)}, bf16[64,3712]{1,0:T(8,128)(2,1)S(1)}, u32[]{:S(2)}, u32[]{:S(2)}) collective-permute-start(bf16[64,3712]{1,0:T(8,128)(2,1)S(1)} %pad_maximum_fusion.1), channel_id=1, source_target_pairs={{0,56},{4,60},{8,0},{12,4},{16,8},{20,12},{24,16},{28,20},{32,24},... | collective-permute-start | bytes 1425416 | tf_op jit(solution)/shard_map/ppermute | solution.py:26
  23.3 9.8 %collective-permute-start.9 = (bf16[48,3712]{1,0:T(8,128)(2,1)S(1)}, bf16[48,3712]{1,0:T(8,128)(2,1)S(1)}, u32[]{:S(2)}, u32[]{:S(2)}) collective-permute-start(bf16[48,3712]{1,0:T(8,128)(2,1)S(1)} %pad_maximum_fusion.7), channel_id=1, source_target_pairs={{0,192},{4,196},{8,200},{12,204},{16,208},{20,212},{24,216},{28,22... | collective-permute-start | bytes 1069064 | tf_op jit(solution)/shard_map/ppermute | solution.py:26
  25.9 10.3 %collective-permute-start.6 = (bf16[48,3712]{1,0:T(8,128)(2,1)S(1)}, bf16[48,3712]{1,0:T(8,128)(2,1)S(1)}, u32[]{:S(2)}, u32[]{:S(2)}) collective-permute-start(bf16[48,3712]{1,0:T(8,128)(2,1)S(1)} %pad_maximum_fusion.6), channel_id=1, source_target_pairs={{0,64},{4,68},{8,72},{12,76},{16,80},{20,84},{24,88},{28,92},{32,9... | collective-permute-start | bytes 1069064 | tf_op jit(solution)/shard_map/ppermute | solution.py:26
  33.2 8.3 %collective-permute-start.10 = (bf16[256,256]{1,0:T(8,128)(2,1)S(1)}, bf16[256,256]{1,0:T(8,128)(2,1)S(1)}, u32[]{:S(2)}, u32[]{:S(2)}) collective-permute-start(bf16[256,256]{1,0:T(8,128)(2,1)S(1)} %pad_maximum_fusion.13.refs_0_), channel_id=1, source_target_pairs={{0,3},{1,0},{2,1},{3,2},{4,7},{5,4},{6,5},{7,6},{8,11},{9,8},{10,9... | collective-permute-start | bytes 393224 | tf_op jit(solution)/shard_map/ppermute | solution.py:34
  36.2 9.5 %copy-start.3 = (bf16[48,3712]{1,0:T(8,128)(2,1)}, bf16[48,3712]{1,0:T(8,128)(2,1)S(1)}, u32[]{:S(2)}) copy-start(bf16[48,3712]{1,0:T(8,128)(2,1)S(1)} %collective-permute-done.6.refs_9_) | copy-start | bytes 1069060
  36.2 5.3 %collective-permute-start.11 = (bf16[256,256]{1,0:T(8,128)(2,1)S(1)}, bf16[256,256]{1,0:T(8,128)(2,1)S(1)}, u32[]{:S(2)}, u32[]{:S(2)}) collective-permute-start(bf16[256,256]{1,0:T(8,128)(2,1)S(1)} %pad_maximum_fusion.13.refs_0_), channel_id=1, source_target_pairs={{0,2},{1,3},{2,0},{3,1},{4,6},{5,7},{6,4},{7,5},{8,10},{9,11},{10,... | collective-permute-start | bytes 393224 | tf_op jit(solution)/shard_map/ppermute | solution.py:34
  39.2 6.5 %collective-permute-start.12 = (bf16[256,256]{1,0:T(8,128)(2,1)S(1)}, bf16[256,256]{1,0:T(8,128)(2,1)S(1)}, u32[]{:S(2)}, u32[]{:S(2)}) collective-permute-start(bf16[256,256]{1,0:T(8,128)(2,1)S(1)} %pad_maximum_fusion.13.refs_0_), channel_id=1, source_target_pairs={{0,1},{1,2},{2,3},{3,0},{4,5},{5,6},{6,7},{7,4},{8,9},{9,10},{10,1... | collective-permute-start | bytes 393224 | tf_op jit(solution)/shard_map/ppermute | solution.py:34
  45.7 1.8 %copy-start.1 = (bf16[4,128,3584]{2,1,0:T(8,128)(2,1)}, bf16[4,128,3584]{2,1,0:T(8,128)(2,1)S(1)}, u32[]{:S(2)}) copy-start(bf16[4,128,3584]{2,1,0:T(8,128)(2,1)S(1)} %collective-permute-done.13.q_other) | copy-start | bytes 11010052
  47.5 21.2 %collective-permute-start.16 = (bf16[64,3712]{1,0:T(8,128)(2,1)S(1)}, bf16[64,3712]{1,0:T(8,128)(2,1)S(1)}, u32[]{:S(2)}, u32[]{:S(2)}) collective-permute-start(bf16[64,3712]{1,0:T(8,128)(2,1)S(1)} %collective-permute-done.8.refs_11_), channel_id=1, source_target_pairs={{0,8},{4,12},{8,16},{12,20},{16,24},{20,28},{24,32},{28,36},{32,40... | collective-permute-start | bytes 1425416 | tf_op jit(solution)/shard_map/ppermute | solution.py:26
  47.6 21.2 %collective-permute-start.15 = (bf16[64,3712]{1,0:T(8,128)(2,1)S(1)}, bf16[64,3712]{1,0:T(8,128)(2,1)S(1)}, u32[]{:S(2)}, u32[]{:S(2)}) collective-permute-start(bf16[64,3712]{1,0:T(8,128)(2,1)S(1)} %collective-permute-done.7.refs_12_), channel_id=1, source_target_pairs={{0,56},{4,60},{8,0},{12,4},{16,8},{20,12},{24,16},{28,20},{32,24},... | collective-permute-start | bytes 1425416 | tf_op jit(solution)/shard_map/ppermute | solution.py:26
  50.5 18.4 %collective-permute-start.17 = (bf16[64,3712]{1,0:T(8,128)(2,1)}, bf16[64,3712]{1,0:T(8,128)(2,1)S(1)}, u32[]{:S(2)}, u32[]{:S(2)}) collective-permute-start(bf16[64,3712]{1,0:T(8,128)(2,1)} %pad_maximum_fusion.3), channel_id=1, source_target_pairs={{0,192},{4,196},{8,200},{12,204},{16,208},{20,212},{24,216},{28,22... | collective-permute-start | bytes 1425416 | tf_op jit(solution)/shard_map/ppermute | solution.py:26
  53.0 15.9 %collective-permute-start.14 = (bf16[64,3712]{1,0:T(8,128)(2,1)}, bf16[64,3712]{1,0:T(8,128)(2,1)S(1)}, u32[]{:S(2)}, u32[]{:S(2)}) collective-permute-start(bf16[64,3712]{1,0:T(8,128)(2,1)} %pad_maximum_fusion.2), channel_id=1, source_target_pairs={{0,64},{4,68},{8,72},{12,76},{16,80},{20,84},{24,88},{28,92},{32,9... | collective-permute-start | bytes 1425416 | tf_op jit(solution)/shard_map/ppermute | solution.py:26
  53.0 3.1 %copy-start = (bf16[4,128,7168]{2,1,0:T(8,128)(2,1)S(1)}, bf16[4,128,7168]{2,1,0:T(8,128)(2,1)}, u32[]{:S(2)}) copy-start(bf16[4,128,7168]{2,1,0:T(8,128)(2,1)} %q_own.3) | copy-start | bytes 22020100
  56.1 2.0 %copy-start.2 = (bf16[4,128,3584]{2,1,0:T(8,128)(2,1)S(1)}, bf16[4,128,3584]{2,1,0:T(8,128)(2,1)}, u32[]{:S(2)}) copy-start(bf16[4,128,3584]{2,1,0:T(8,128)(2,1)} %copy-done.1) | copy-start | bytes 11010052
  58.2 1.0 copy-start.4
  69.1 18.1 %copy-start.5 = (s32[64]{0:T(128)S(1)}, s32[64]{0:T(128)}, u32[]{:S(2)}) copy-start(s32[64]{0:T(128)} %constant.92.clone) | copy-start | bytes 772
  69.1 18.1 %copy-start.6 = (s32[64]{0:T(128)S(1)}, s32[64]{0:T(128)}, u32[]{:S(2)}) copy-start(s32[64]{0:T(128)} %constant.93.clone) | copy-start | bytes 772
  69.1 18.1 %copy-start.7 = (s32[64]{0:T(128)S(1)}, s32[64]{0:T(128)}, u32[]{:S(2)}) copy-start(s32[64]{0:T(128)} %constant.94.clone) | copy-start | bytes 772
  69.1 12.4 %collective-permute-start.19 = (bf16[48,3712]{1,0:T(8,128)(2,1)S(1)}, bf16[48,3712]{1,0:T(8,128)(2,1)S(1)}, u32[]{:S(2)}, u32[]{:S(2)}) collective-permute-start(bf16[48,3712]{1,0:T(8,128)(2,1)S(1)} %slice.170), channel_id=1, source_target_pairs={{0,56},{4,60},{8,0},{12,4},{16,8},{20,12},{24,16},{28,20},{32,24},... | collective-permute-start | bytes 1069064 | tf_op jit(solution)/shard_map/ppermute | solution.py:26
  69.3 12.4 %collective-permute-start.18 = (bf16[64,3712]{1,0:T(8,128)(2,1)S(1)}, bf16[64,3712]{1,0:T(8,128)(2,1)S(1)}, u32[]{:S(2)}, u32[]{:S(2)}) collective-permute-start(bf16[64,3712]{1,0:T(8,128)(2,1)S(1)} %pad_maximum_fusion.4), channel_id=1, source_target_pairs={{0,64},{4,68},{8,72},{12,76},{16,80},{20,84},{24,88},{28,92},{32,9... | collective-permute-start | bytes 1425416 | tf_op jit(solution)/shard_map/ppermute | solution.py:26
  69.3 12.3 %collective-permute-start.21 = (bf16[64,3712]{1,0:T(8,128)(2,1)S(1)}, bf16[64,3712]{1,0:T(8,128)(2,1)S(1)}, u32[]{:S(2)}, u32[]{:S(2)}) collective-permute-start(bf16[64,3712]{1,0:T(8,128)(2,1)S(1)} %pad_maximum_fusion.5), channel_id=1, source_target_pairs={{0,192},{4,196},{8,200},{12,204},{16,208},{20,212},{24,216},{28,22... | collective-permute-start | bytes 1425416 | tf_op jit(solution)/shard_map/ppermute | solution.py:26
  72.1 9.5 %collective-permute-start.20 = (bf16[48,3712]{1,0:T(8,128)(2,1)S(1)}, bf16[48,3712]{1,0:T(8,128)(2,1)S(1)}, u32[]{:S(2)}, u32[]{:S(2)}) collective-permute-start(bf16[48,3712]{1,0:T(8,128)(2,1)S(1)} %pad_maximum_fusion.8), channel_id=1, source_target_pairs={{0,8},{4,12},{8,16},{12,20},{16,24},{20,28},{24,32},{28,36},{32,40... | collective-permute-start | bytes 1069064 | tf_op jit(solution)/shard_map/ppermute | solution.py:26
  81.8 13.4 %collective-permute-start.22 = (bf16[32,3712]{1,0:T(8,128)(2,1)S(1)}, bf16[32,3712]{1,0:T(8,128)(2,1)S(1)}, u32[]{:S(2)}, u32[]{:S(2)}) collective-permute-start(bf16[32,3712]{1,0:T(8,128)(2,1)S(1)} %get-tuple-element.64), channel_id=1, source_target_pairs={{0,64},{4,68},{8,72},{12,76},{16,80},{20,84},{24,88},{28,92},{32,9... | collective-permute-start | bytes 712712 | tf_op jit(solution)/shard_map/ppermute | solution.py:26
  81.9 13.3 %collective-permute-start.23 = (bf16[32,3712]{1,0:T(8,128)(2,1)S(1)}, bf16[32,3712]{1,0:T(8,128)(2,1)S(1)}, u32[]{:S(2)}, u32[]{:S(2)}) collective-permute-start(bf16[32,3712]{1,0:T(8,128)(2,1)S(1)} %get-tuple-element.65), channel_id=1, source_target_pairs={{0,192},{4,196},{8,200},{12,204},{16,208},{20,212},{24,216},{28,22... | collective-permute-start | bytes 712712 | tf_op jit(solution)/shard_map/ppermute | solution.py:26
  84.5 10.6 %collective-permute-start.24 = (bf16[32,3712]{1,0:T(8,128)(2,1)S(1)}, bf16[32,3712]{1,0:T(8,128)(2,1)S(1)}, u32[]{:S(2)}, u32[]{:S(2)}) collective-permute-start(bf16[32,3712]{1,0:T(8,128)(2,1)S(1)} %get-tuple-element.66), channel_id=1, source_target_pairs={{0,8},{4,12},{8,16},{12,20},{16,24},{20,28},{24,32},{28,36},{32,40... | collective-permute-start | bytes 712712 | tf_op jit(solution)/shard_map/ppermute | solution.py:26
  84.6 10.6 %collective-permute-start.25 = (bf16[32,3712]{1,0:T(8,128)(2,1)S(1)}, bf16[32,3712]{1,0:T(8,128)(2,1)S(1)}, u32[]{:S(2)}, u32[]{:S(2)}) collective-permute-start(bf16[32,3712]{1,0:T(8,128)(2,1)S(1)} %get-tuple-element.67), channel_id=1, source_target_pairs={{0,56},{4,60},{8,0},{12,4},{16,8},{20,12},{24,16},{28,20},{32,24},... | collective-permute-start | bytes 712712 | tf_op jit(solution)/shard_map/ppermute | solution.py:26
  87.2 10.6 %collective-permute-start.26 = (bf16[32,3712]{1,0:T(8,128)(2,1)S(1)}, bf16[32,3712]{1,0:T(8,128)(2,1)S(1)}, u32[]{:S(2)}, u32[]{:S(2)}) collective-permute-start(bf16[32,3712]{1,0:T(8,128)(2,1)S(1)} %concatenate.103), channel_id=1, source_target_pairs={{0,72},{4,76},{8,80},{12,84},{16,88},{20,92},{24,96},{28,100},{32,... | collective-permute-start | bytes 712712 | tf_op jit(solution)/shard_map/ppermute | solution.py:26
